TPU v7x, 32 devices: a whole 2x2x4 slice. The times are simulated.
32 devices in a mesh: dp: 4 (over z), fsdp: 8 (over y, x, core).
Axes of the slice: x: 2, y: 2, z: 4, core: 2. Of those that a mesh axis runs over, the one named last changes fastest.
Arguments:
- tokens: bfloat16 [98304, 512], P(('dp', 'fsdp')), may hold values from -6 to 6
- lengths: int32 [96], P(('dp', 'fsdp')), may hold values from 256 to 1024, as said below
- w_query: bfloat16 [512, 512], P(None, ('dp', 'fsdp')), may hold values from -0.25 to 0.25
- w_key: bfloat16 [512, 512], P(None, ('dp', 'fsdp')), may hold values from -0.25 to 0.25
- w_value: bfloat16 [512, 512], P(None, ('dp', 'fsdp')), may hold values from -0.25 to 0.25
- w_out: bfloat16 [512, 512], P(None, ('dp', 'fsdp')), may hold values from -6 to 6
- w_up: bfloat16 [512, 2048], P(None, ('dp', 'fsdp')), may hold values from -0.25 to 0.25
- w_down: bfloat16 [2048, 512], P(None, ('dp', 'fsdp')), may hold values from -0.125 to 0.125
- bias_up: bfloat16 [2048], P(('dp', 'fsdp')), may hold values from -3 to 3
- bias_down: bfloat16 [512], P(('dp', 'fsdp')), may hold values from -4 to 4
- gain_attn: bfloat16 [512], P(('dp', 'fsdp')), may hold values from 0.099609375 to 1.8984375
- shift_attn: bfloat16 [512], P(('dp', 'fsdp')), may hold values from -3 to 3
- gain_ffn: bfloat16 [512], P(('dp', 'fsdp')), may hold values from 0.099609375 to 1.8984375
- shift_ffn: bfloat16 [512], P(('dp', 'fsdp')), may hold values from -3 to 3
- cotangent: bfloat16 [98304, 512], P(('dp', 'fsdp')), may hold values from -0.0390625 to 0.0390625
Outputs:
- output: bfloat16 [98304, 512], P(('dp', 'fsdp'))
- grad_tokens: bfloat16 [98304, 512], P(('dp', 'fsdp'))
- grad_w_query: float32 [512, 512], P(None, ('dp', 'fsdp'))
- grad_w_key: float32 [512, 512], P(None, ('dp', 'fsdp'))
- grad_w_value: float32 [512, 512], P(None, ('dp', 'fsdp'))
- grad_w_out: float32 [512, 512], P(None, ('dp', 'fsdp'))
- grad_w_up: float32 [512, 2048], P(None, ('dp', 'fsdp'))
- grad_w_down: float32 [2048, 512], P(None, ('dp', 'fsdp'))
- grad_bias_up: float32 [2048], P(('dp', 'fsdp'))
- grad_bias_down: float32 [512], P(('dp', 'fsdp'))
- grad_gain_attn: float32 [512], P(('dp', 'fsdp'))
- grad_shift_attn: float32 [512], P(('dp', 'fsdp'))
- grad_gain_ffn: float32 [512], P(('dp', 'fsdp'))
- grad_shift_ffn: float32 [512], P(('dp', 'fsdp'))
Inputs may be any that keep to these rules, and one draw needn't show every extreme that they name: `lengths`: each entry is the number of real tokens at the start of a sequence slot of 1024; the rest of the slot is padding. Both ends of the range are taken in every draw.
All inputs are finite; a program needn't handle non-finite values.
Results may differ from a plain program's by a relative error of at most 0.03.
Values may be sent and summed in bfloat16 or wider, within the bound.
No kernel may reach another device: no remote copies, remote signals or barrier semaphores. Data moves between devices by JAX's collectives and lax.ppermute only.
A program may use at most 512 MiB of HBM per device.

v0:
```python
import functools

import jax
import jax.numpy as jnp
import numpy as np
from jax import lax
from jax.experimental import pallas as pl
from jax.experimental.pallas import tpu as pltpu
from jax.sharding import PartitionSpec as P

D = 512
H = 8
DH = 64
FF = 2048
BLOCK = 16
LEVELS = 6
LEN = 1024
AXES = ("dp", "fsdp")
BF16 = jnp.bfloat16
F32 = jnp.float32

STARTS = (32, 1072, 1600, 1872, 2016, 2096)
SIZES = tuple(LEN >> level for level in range(LEVELS))
ROWS = 2192
GAPS = ((0, 32), (1056, 16), (1584, 16), (1856, 16), (2000, 16), (2080, 16), (2128, 64))
WINDOWS = 32
QUERIES = 64
KEYS = 128
POOL_CHUNK = 256
SHARE = 16
FIRST_ROWS = 3 * SHARE + 8
SECOND_ROWS = 9 * SHARE + 8
SCORE = 0.125 * 1.4426950408889634


def nn(left, right):
    return lax.dot_general(left, right, (((1,), (0,)), ((), ())), preferred_element_type=F32)


def nt(left, right):
    return lax.dot_general(left, right, (((1,), (1,)), ((), ())), preferred_element_type=F32)


def tn(left, right):
    return lax.dot_general(left, right, (((0,), (0,)), ((), ())), preferred_element_type=F32)


def score_bias():
    query = (np.arange(2 * QUERIES) % QUERIES)[:, None]
    key = np.arange(KEYS)[None, :] - 32
    near = np.abs(query // 16 - key // 16) <= 1
    apart = np.abs(query // 8 - key // 8) > 1
    return np.where(np.stack([near, near & apart]), 0.0, -1e30).astype(np.float32)


def pool_matrix():
    matrix = np.zeros((POOL_CHUNK, POOL_CHUNK), np.float32)
    first = 0
    for level in range(1, LEVELS):
        count = POOL_CHUNK >> level
        for row in range(count):
            matrix[first + row, row << level : (row + 1) << level] = 0.5**level
        first += count
    return matrix


def halves():
    lane = np.arange(128)
    return np.stack([lane < DH, lane >= DH]).astype(np.float32)


def window_loop(step):
    for window in range(WINDOWS):
        gaps = sum(window >= first for first in (16, 24, 28, 30, 31))
        row = STARTS[0] + QUERIES * window + 16 * gaps
        step(
            pl.ds(row, QUERIES),
            pl.ds(row - 32, KEYS),
            pl.ds(window * 2 * QUERIES, 2 * QUERIES),
            int(window >= 16),
        )


def row_loop(total, size, step):
    for first in range(0, total, size):
        step(first)


def row_fori(total, size, step, unroll):
    def body(index, carry):
        for inner in range(unroll):
            step(pl.multiple_of((index * unroll + inner) * size, size))
        return carry

    lax.fori_loop(0, total // (size * unroll), body, 0)


def pair_lanes(pair):
    return slice(128 * pair, 128 * pair + 128)


def by_head(values, half):
    return jnp.concatenate([values * half[0:1, :], values * half[1:2, :]], axis=0)


def joined_heads(values, low_head):
    return jnp.where(low_head, values[:QUERIES], values[QUERIES:])


def fill_counts(counts, length):
    clear_gaps(counts)
    for level in range(LEVELS):
        place = lax.broadcasted_iota(jnp.int32, (SIZES[level], 128), 0)
        span = 1 << level
        number = jnp.clip(length - place * span, 0, span).astype(F32)
        counts[STARTS[level] : STARTS[level] + SIZES[level], :] = number.astype(BF16)


def block_places(place, plain, sign):
    for half in range(2):
        for block in range(16):
            if plain:
                yield half, block, half * 16 + block
            else:
                column = place[1] ^ (half + 2 * (block // 4))
                row = (place[0] + 4 + sign * (block % 4)) % 4
                yield half, block, row * 8 + column


def sixteen(device):
    return pl.ds(pl.multiple_of(device * SHARE, SHARE), SHARE)


def sixty_four(device):
    return pl.ds(pl.multiple_of(device * 4 * SHARE, 4 * SHARE), 4 * SHARE)


def load_first(place, plain, blocks, weights, vectors):
    total = jnp.zeros((8, D), F32)
    for half, block, device in block_places(place, plain, -1):
        source = blocks[half]
        for part in range(3):
            rows = pl.ds(pl.multiple_of(part * D + device * SHARE, SHARE), SHARE)
            weights[rows, :] = source[block, part * SHARE : part * SHARE + SHARE, :]
        total = total + source[block, 3 * SHARE : 3 * SHARE + 8, :].astype(F32)
    vectors[...] = total


def load_second(place, plain, blocks, w_out, w_up, w_down, vectors):
    total = jnp.zeros((8, D), F32)
    for half, block, device in block_places(place, plain, -1):
        source = blocks[half]
        w_out[sixteen(device), :] = source[block, 0:SHARE, :]
        w_up[sixty_four(device), :] = source[block, SHARE : 5 * SHARE, :]
        for part in range(4):
            at = (5 + part) * SHARE
            w_down[part, sixteen(device), :] = source[block, at : at + SHARE, :]
        total = total + source[block, 9 * SHARE : 9 * SHARE + 8, :].astype(F32)
    vectors[...] = total


def layer_norm(values):
    mean = jnp.mean(values, axis=-1, keepdims=True)
    centred = values - mean
    inverse = lax.rsqrt(jnp.mean(centred * centred, axis=-1, keepdims=True) + 1e-05)
    return centred * inverse, inverse


def norm_back(gradient, normed, inverse, gain):
    scaled = gradient * gain
    return inverse * (
        scaled
        - jnp.mean(scaled, axis=-1, keepdims=True)
        - normed * jnp.mean(scaled * normed, axis=-1, keepdims=True)
    )


def clear_gaps(ref):
    for first, count in GAPS:
        ref[first : first + count, :] = jnp.zeros((count, ref.shape[1]), ref.dtype)


def spread_up(ref, factor):
    for level in range(LEVELS - 2, -1, -1):
        count = SIZES[level + 1]
        size = min(count, 64)

        def step(first, level=level, size=size):
            for pair in range(4):
                above = ref[pair, pl.ds(STARTS[level + 1] + first, size), :]
                if factor != 1.0:
                    above = above * factor
                for odd in (0, 1):
                    below = pl.ds(STARTS[level] + 2 * first + odd, size, stride=2)
                    ref[pair, below, :] = ref[pair, below, :] + above

        row_loop(count, size, step)


def attend_kernel(
    plain,
    lengths,
    place,
    tokens,
    near_blocks,
    far_blocks,
    bias,
    pool,
    half,
    query,
    key,
    value,
    probs,
    attn,
    total,
    weights,
    vectors,
    normed,
    joined,
    top,
    counts,
    numer,
    denom,
):
    @pl.when(pl.program_id(0) == 0)
    def _():
        load_first(place, plain, (near_blocks, far_blocks), weights, vectors)

    length = lengths[pl.program_id(0)]
    gain = vectors[0:1, :]
    shift = vectors[1:2, :]

    def norm_step(first):
        rows = pl.ds(first, 64)
        values, _ = layer_norm(tokens[rows, :].astype(F32))
        normed[rows, :] = (values * gain + shift).astype(BF16)

    row_loop(LEN, 64, norm_step)
    for ref in (query, key, value):
        clear_gaps(ref)
    fill_counts(counts, length)
    targets = ((query, 0), (key, D), (value, 2 * D))
    for first in range(0, LEN, POOL_CHUNK):
        rows = slice(first, first + POOL_CHUNK)
        chunk = first // POOL_CHUNK
        values = nt(normed[rows, :], weights[...])
        valid = (lax.broadcasted_iota(jnp.int32, (POOL_CHUNK, 1), 0) + first < length).astype(F32)
        joined[rows, : 2 * D] = values[:, : 2 * D].astype(BF16)
        joined[rows, 2 * D :] = (values[:, 2 * D :] * valid).astype(BF16)
        pooled = nn(pool[...], joined[rows, :])
        for ref, lane in targets:
            start = STARTS[0] + first
            ref[start : start + POOL_CHUNK, :] = joined[rows, lane : lane + D]
            at = 0
            for level in range(1, LEVELS):
                count = POOL_CHUNK >> level
                part = pooled[at : at + count, lane : lane + D]
                at += count
                if ref is value:
                    part = part * float(1 << level)
                if level < LEVELS - 1:
                    start = STARTS[level] + chunk * count
                    ref[start : start + count, :] = part.astype(BF16)
                else:
                    top[chunk * count : chunk * count + count, lane : lane + D] = part
    for ref, lane in targets:
        ref[STARTS[-1] : STARTS[-1] + SIZES[-1], :] = top[:, lane : lane + D].astype(BF16)

    def score_step(rows, near, flat, kind):
        allowed = bias[kind]
        for pair in range(4):
            lanes = pair_lanes(pair)
            scores = nt(by_head(query[rows, lanes], half), key[near, lanes])
            probs[flat, lanes] = jnp.exp2(scores * SCORE + allowed).astype(BF16)

    window_loop(score_step)
    low_head = lax.broadcasted_iota(jnp.int32, (QUERIES, 128), 1) < DH

    def value_step(rows, near, flat, kind):
        number = counts[near, :]
        for pair in range(4):
            lanes = pair_lanes(pair)
            both = nn(probs[flat, lanes], jnp.concatenate([value[near, lanes], number], axis=1))
            numer[pair, rows, :] = joined_heads(both[:, :128], low_head)
            denom[pair, rows, :] = joined_heads(both[:, 128:], low_head)

    window_loop(value_step)
    spread_up(numer, 1.0)
    spread_up(denom, 1.0)

    def join_step(first):
        rows = pl.ds(first, 64)
        inner = pl.ds(STARTS[0] + first, 64)
        for pair in range(4):
            lanes = pair_lanes(pair)
            below = denom[pair, inner, :]
            attn[rows, lanes] = (numer[pair, inner, :] / below).astype(BF16)
            total[rows, lanes] = below

    row_loop(LEN, 64, join_step)


def feed_kernel(
    plain,
    place,
    tokens,
    attn,
    total,
    cotangent,
    near_blocks,
    far_blocks,
    output,
    middle_grad,
    numer_grad,
    total_grad,
    grads_0,
    grads_1,
    grads_2,
    grads_3,
    w_out,
    w_up,
    w_down,
    vectors,
    middle,
    normed,
    inverse,
    normed_low,
    hidden,
    result,
    gathered,
    active,
    back,
    sums,
    acc_out,
    acc_up,
    acc_down,
):
    @pl.when(pl.program_id(0) == 0)
    def _():
        acc_out[...] = jnp.zeros_like(acc_out)
        acc_up[...] = jnp.zeros_like(acc_up)
        acc_down[...] = jnp.zeros_like(acc_down)
        sums[...] = jnp.zeros_like(sums)
        load_second(place, plain, (near_blocks, far_blocks), w_out, w_up, w_down, vectors)

    gain = vectors[0:1, :]
    shift = vectors[1:2, :]
    bias_down = vectors[2:3, :]
    middle[...] = nt(attn[...], w_out[...])

    def norm_step(first):
        rows = pl.ds(first, 64)
        values = middle[rows, :] + tokens[rows, :].astype(F32)
        middle[rows, :] = values
        norm, factor = layer_norm(values)
        normed[rows, :] = norm
        inverse[rows, :] = jnp.broadcast_to(factor, (64, 128))
        normed_low[rows, :] = (norm * gain + shift).astype(BF16)

    row_loop(LEN, 64, norm_step)
    gathered[...] = jnp.zeros_like(gathered)

    def part_step(part, carry):
        up = w_up[pl.ds(pl.multiple_of(part * D, D), D), :]
        down = w_down[part]
        bias_up = vectors[pl.ds(3 + part, 1), :]
        count = jnp.zeros((8, D), F32)
        for start in range(0, LEN, 512):
            wide = slice(start, start + 512)
            hidden[wide, :] = nt(normed_low[wide, :], up)
            result[wide, :] = nn(cotangent[wide, :], down)
            for first in range(start, start + 512, 64):
                rows = slice(first, first + 64)
                value = hidden[rows, :] + bias_up
                gate = 0.5 * jnp.tanh(0.5 * value) + 0.5
                active[rows, :] = (value * gate).astype(BF16)
                slope = gate * (1.0 + value * (1.0 - gate))
                gradient = (result[rows, :] * slope).astype(BF16)
                back[rows, :] = gradient
                count = count + jnp.sum(gradient.astype(F32).reshape(8, 8, D), axis=0)
        for start in range(0, LEN, 512):
            wide = slice(start, start + 512)
            middle[wide, :] += nt(active[wide, :], down)
            gathered[wide, :] += nn(back[wide, :], up)
        sums[pl.ds(pl.multiple_of(24 + 8 * part, 8), 8), :] += count
        acc_down[part] += tn(cotangent[...], active[...])
        acc_up[pl.ds(pl.multiple_of(part * D, D), D), :] += tn(back[...], normed_low[...])
        return carry

    lax.fori_loop(0, FF // D, part_step, 0)

    def back_step(first):
        rows = pl.ds(first, 64)
        output[rows, :] = (middle[rows, :] + bias_down).astype(BF16)
        gradient = gathered[rows, :]
        norm = normed[rows, :]
        value = cotangent[rows, :].astype(F32)
        sums[0:8, :] += jnp.sum((gradient * norm).reshape(8, 8, D), axis=0)
        sums[8:16, :] += jnp.sum(gradient.reshape(8, 8, D), axis=0)
        sums[16:24, :] += jnp.sum(value.reshape(8, 8, D), axis=0)
        value = value + norm_back(gradient, norm, inverse[rows, 0:1], gain)
        middle_grad[rows, :] = value.astype(BF16)

    row_loop(LEN, 64, back_step)
    acc_out[...] += tn(middle_grad[...], attn[...])
    gathered[...] = nn(middle_grad[...], w_out[...])

    def numer_step(first):
        rows = pl.ds(first, 64)
        gradient = gathered[rows, :].astype(BF16).astype(F32) / total[rows, :]
        numer_grad[rows, :] = gradient.astype(BF16)
        total_grad[rows, :] = (-gradient * attn[rows, :].astype(F32)).astype(BF16)

    row_loop(LEN, 64, numer_step)

    @pl.when(pl.program_id(0) == pl.num_programs(0) - 1)
    def _():
        small = jnp.sum(sums[...].reshape(7, 8, D), axis=1)
        small = jnp.concatenate([small, jnp.zeros((1, D), F32)], axis=0).astype(BF16)
        for half, block, device in block_places(place, plain, 1):
            target = (grads_0, grads_1, grads_2, grads_3)[block // 4]
            into = 4 * half + block % 4
            target[into, 0:SHARE, :] = acc_out[sixteen(device), :].astype(BF16)
            target[into, SHARE : 5 * SHARE, :] = acc_up[sixty_four(device), :].astype(BF16)
            for part in range(4):
                at = (5 + part) * SHARE
                target[into, at : at + SHARE, :] = acc_down[part, sixteen(device), :].astype(BF16)
            target[into, 9 * SHARE : 9 * SHARE + 8, :] = small


def attend_back_kernel(
    plain,
    lengths,
    place,
    tokens,
    middle_grad,
    numer_grad,
    total_grad,
    query,
    key,
    value,
    probs,
    weights,
    vectors,
    pool,
    half,
    grad_tokens,
    near_grads,
    far_grads,
    numer,
    denom,
    score_grad,
    total,
    joined,
    normed,
    counts,
    top,
    sums,
    acc,
):
    step_index = pl.program_id(0)
    length = lengths[step_index]

    @pl.when(step_index == 0)
    def _():
        acc[...] = jnp.zeros_like(acc)
        sums[...] = jnp.zeros_like(sums)

    gain = vectors[0:1, :]
    shift = vectors[1:2, :]
    clear_gaps(numer)
    clear_gaps(denom)
    fill_counts(counts, length)
    for source, target in ((numer_grad, numer), (total_grad, denom)):
        target[STARTS[0] : STARTS[0] + LEN, :] = source[...]
        for first in range(0, LEN, POOL_CHUNK):
            chunk = first // POOL_CHUNK
            pooled = nn(pool[...], source[first : first + POOL_CHUNK, :])
            at = 0
            for level in range(1, LEVELS):
                count = POOL_CHUNK >> level
                part = pooled[at : at + count] * float(1 << level)
                at += count
                if level < LEVELS - 1:
                    start = STARTS[level] + chunk * count
                    target[start : start + count, :] = part.astype(BF16)
                else:
                    top[chunk * count : chunk * count + count, :] = part
        target[STARTS[-1] : STARTS[-1] + SIZES[-1], :] = top[...].astype(BF16)

    def score_step(rows, near, flat, kind):
        number = counts[near, :]
        for pair in range(4):
            lanes = pair_lanes(pair)
            left = jnp.concatenate(
                [by_head(numer[rows, lanes], half), by_head(denom[rows, lanes], half)], axis=1
            )
            right = jnp.concatenate([value[near, lanes], number], axis=1)
            score_grad[flat, lanes] = (nt(left, right) * probs[flat, lanes].astype(F32)).astype(BF16)

    window_loop(score_step)
    low_head = lax.broadcasted_iota(jnp.int32, (QUERIES, 128), 1) < DH

    def query_step(rows, near, flat, kind):
        for pair in range(4):
            lanes = pair_lanes(pair)
            both = nn(score_grad[flat, lanes], key[near, lanes])
            total[pair, rows, :] = joined_heads(both, low_head)

    window_loop(query_step)
    spread_up(total, 0.5)

    def take(at, scale, masked):
        def take_step(first):
            rows = pl.ds(first, 64)
            if masked:
                place = lax.broadcasted_iota(jnp.int32, (64, 1), 0) + first
                valid = (place < length).astype(F32)
            for pair in range(4):
                values = total[pair, pl.ds(STARTS[0] + first, 64), :]
                if scale != 1.0:
                    values = values * scale
                if masked:
                    values = values * valid
                joined[rows, at + 128 * pair : at + 128 * pair + 128] = values.astype(BF16)

        row_loop(LEN, 64, take_step)

    take(0, 0.125, False)
    for at, left, right, factor, scale, masked in (
        (D, score_grad, query, 0.5, 0.125, False),
        (2 * D, probs, numer, 1.0, 1.0, True),
    ):
        total[...] = jnp.zeros_like(total)

        def near_step(rows, near, flat, kind, left=left, right=right):
            for pair in range(4):
                lanes = pair_lanes(pair)
                total[pair, near, :] += tn(left[flat, lanes], by_head(right[rows, lanes], half))

        window_loop(near_step)
        spread_up(total, factor)
        take(at, scale, masked)

    def norm_step(first):
        rows = pl.ds(first, 64)
        values, _ = layer_norm(tokens[rows, :].astype(F32))
        normed[rows, :] = (values * gain + shift).astype(BF16)

    row_loop(LEN, 64, norm_step)
    for part in range(3):
        lanes = slice(D * part, D * part + D)
        acc[lanes, :] += tn(joined[:, lanes], normed[...])
    for first in range(0, LEN, POOL_CHUNK):
        rows = slice(first, first + POOL_CHUNK)
        passed = nn(joined[rows, :], weights[...])
        for pair in range(4):
            total[pair, rows, :] = passed[:, pair_lanes(pair)]

    def back_step(first):
        rows = pl.ds(first, 64)
        norm, inverse = layer_norm(tokens[rows, :].astype(F32))
        gradient = jnp.concatenate([total[pair, rows, :] for pair in range(4)], axis=1)
        sums[0:8, :] += jnp.sum((gradient * norm).reshape(8, 8, D), axis=0)
        sums[8:16, :] += jnp.sum(gradient.reshape(8, 8, D), axis=0)
        value = middle_grad[rows, :].astype(F32) + norm_back(gradient, norm, inverse, gain)
        grad_tokens[rows, :] = value.astype(BF16)

    row_loop(LEN, 64, back_step)

    @pl.when(step_index == pl.num_programs(0) - 1)
    def _():
        small = jnp.sum(sums[...].reshape(2, 8, D), axis=1)
        small = jnp.concatenate([small, jnp.zeros((6, D), F32)], axis=0).astype(BF16)
        for side, block, device in block_places(place, plain, 1):
            target = (near_grads, far_grads)[side]
            for part in range(3):
                rows = pl.ds(pl.multiple_of(part * D + device * SHARE, SHARE), SHARE)
                target[block, part * SHARE : part * SHARE + SHARE, :] = acc[rows, :].astype(BF16)
            target[block, 3 * SHARE : 3 * SHARE + 8, :] = small


SMEM = pl.BlockSpec(memory_space=pltpu.SMEM)


def whole(*shape):
    return pl.BlockSpec(shape, lambda i: (0,) * len(shape), pipeline_mode=pl.Buffered(1))


def per_sequence(rows, columns):
    return pl.BlockSpec((rows, columns), lambda i: (i, 0))


def vmem(rows, columns, dtype):
    return pltpu.VMEM((rows, columns), dtype)


def shape_of(rows, columns, dtype):
    return jax.ShapeDtypeStruct((rows, columns), dtype)


PARAMS = pltpu.CompilerParams(
    dimension_semantics=("arbitrary",), vmem_limit_bytes=63 * 1024 * 1024
)


def cost(microseconds):
    return pl.CostEstimate(
        flops=int(microseconds * 1.0e9), bytes_accessed=int(microseconds * 1.0e6), transcendentals=0
    )


def attend(lengths, place, plain, tokens, blocks):
    count = lengths.shape[0]
    levels = shape_of(count * ROWS, D, BF16)
    one = per_sequence(LEN, D)
    all_levels = per_sequence(ROWS, D)
    flat = WINDOWS * 2 * QUERIES
    return pl.pallas_call(
        functools.partial(attend_kernel, plain),
        grid=(count,),
        in_specs=[
            SMEM,
            SMEM,
            one,
            whole(16, FIRST_ROWS, D),
            whole(16, FIRST_ROWS, D),
            whole(2, 2 * QUERIES, KEYS),
            whole(POOL_CHUNK, POOL_CHUNK),
            whole(2, 128),
        ],
        out_specs=[all_levels] * 3
        + [per_sequence(flat, D), one, one, whole(3 * D, D), whole(8, D)],
        out_shape=[levels] * 3
        + [
            shape_of(count * flat, D, BF16),
            shape_of(count * LEN, D, BF16),
            shape_of(count * LEN, D, F32),
            shape_of(3 * D, D, BF16),
            shape_of(8, D, F32),
        ],
        scratch_shapes=[
            vmem(LEN, D, BF16),
            vmem(LEN, 3 * D, BF16),
            vmem(SIZES[-1], 3 * D, F32),
            vmem(ROWS, 128, BF16),
            pltpu.VMEM((4, ROWS, 128), F32),
            pltpu.VMEM((4, ROWS, 128), F32),
        ],
        compiler_params=PARAMS,
        cost_estimate=cost(40),
        name="attend",
    )(
        lengths,
        place,
        tokens,
        *blocks,
        jnp.asarray(score_bias()),
        jnp.asarray(pool_matrix(), BF16),
        jnp.asarray(halves(), BF16),
    )


def feed(place, plain, tokens, attn, total, cotangent, blocks):
    rows = tokens.shape[0]
    one = per_sequence(LEN, D)
    low = shape_of(rows, D, BF16)
    grads = whole(8, SECOND_ROWS, D)
    return pl.pallas_call(
        functools.partial(feed_kernel, plain),
        grid=(rows // LEN,),
        in_specs=[SMEM] + [one] * 4 + [whole(16, SECOND_ROWS, D)] * 2,
        out_specs=[one] * 4 + [grads] * 4,
        out_shape=[low] * 4 + [jax.ShapeDtypeStruct((8, SECOND_ROWS, D), BF16)] * 4,
        scratch_shapes=[
            vmem(D, D, BF16),
            vmem(FF, D, BF16),
            pltpu.VMEM((4, D, D), BF16),
            vmem(8, D, F32),
            vmem(LEN, D, F32),
            vmem(LEN, D, F32),
            vmem(LEN, 128, F32),
            vmem(LEN, D, BF16),
            vmem(LEN, D, F32),
            vmem(LEN, D, F32),
            vmem(LEN, D, F32),
            vmem(LEN, D, BF16),
            vmem(LEN, D, BF16),
            vmem(56, D, F32),
            vmem(D, D, F32),
            vmem(FF, D, F32),
            pltpu.VMEM((4, D, D), F32),
        ],
        compiler_params=PARAMS,
        cost_estimate=cost(75),
        name="feed",
    )(place, tokens, attn, total, cotangent, *blocks)


def attend_back(lengths, place, plain, tokens, middle_grad, numer_grad, total_grad, kept):
    count = lengths.shape[0]
    one = per_sequence(LEN, D)
    all_levels = per_sequence(ROWS, D)
    flat = WINDOWS * 2 * QUERIES
    grads = whole(16, FIRST_ROWS, D)
    return pl.pallas_call(
        functools.partial(attend_back_kernel, plain),
        grid=(count,),
        in_specs=[SMEM, SMEM]
        + [one] * 4
        + [all_levels] * 3
        + [per_sequence(flat, D)]
        + [whole(3 * D, D), whole(8, D), whole(POOL_CHUNK, POOL_CHUNK), whole(2, 128)],
        out_specs=[one, grads, grads],
        out_shape=[shape_of(count * LEN, D, BF16)]
        + [jax.ShapeDtypeStruct((16, FIRST_ROWS, D), BF16)] * 2,
        scratch_shapes=[
            vmem(ROWS, D, BF16),
            vmem(ROWS, D, BF16),
            vmem(flat, D, BF16),
            pltpu.VMEM((4, ROWS, 128), F32),
            vmem(LEN, 3 * D, BF16),
            vmem(LEN, D, BF16),
            vmem(ROWS, 128, BF16),
            vmem(SIZES[-1], D, F32),
            vmem(16, D, F32),
            vmem(3 * D, D, F32),
        ],
        compiler_params=PARAMS,
        cost_estimate=cost(60),
        name="attend_back",
    )(
        lengths,
        place,
        tokens,
        middle_grad,
        numer_grad,
        total_grad,
        *kept,
        jnp.asarray(pool_matrix(), BF16),
        jnp.asarray(halves(), BF16),
    )


def pack_kernel(place, *refs):
    w_query, w_key, w_value, w_out, w_up, w_down, bias_up, bias_down, *norms, first, second = refs
    for part, ref in enumerate((w_query, w_key, w_value)):
        first[part * SHARE : part * SHARE + SHARE, :] = ref[...]
    second[0:SHARE, :] = w_out[...]
    second[SHARE : 5 * SHARE, :] = w_up[...]
    for part in range(4):
        at = (5 + part) * SHARE
        second[at : at + SHARE, :] = w_down[:, D * part : D * part + D]
    device = place[0] * 8 + place[1]
    lane = lax.broadcasted_iota(jnp.int32, (SHARE, D), 1)
    mine = lane == lax.broadcasted_iota(jnp.int32, (SHARE, D), 0) + device * SHARE
    mine = mine.astype(F32).astype(BF16)
    gain_attn, shift_attn, gain_ffn, shift_ffn = norms
    row = lax.broadcasted_iota(jnp.int32, (8, D), 0)

    def rows_of(vectors):
        total = jnp.zeros((8, D), F32)
        for place_of, vector in enumerate(vectors):
            total = jnp.where(row == place_of, nn(vector[...], mine), total)
        return total

    first[3 * SHARE :, :] = rows_of((gain_attn, shift_attn)).astype(BF16)
    lane = lax.broadcasted_iota(jnp.int32, (4 * SHARE, D), 1)
    mine_up = lane == lax.broadcasted_iota(jnp.int32, (4 * SHARE, D), 0) + (device % 8) * 4 * SHARE
    wide = nn(bias_up[...], mine_up.astype(F32).astype(BF16))
    vectors = rows_of((gain_ffn, shift_ffn, bias_down))
    second[9 * SHARE :, :] = jnp.where(row == 3 + device // 8, wide, vectors).astype(BF16)


def pack(place, weights, vectors):
    operands = [w.T for w in weights] + [v.reshape(1, -1) for v in vectors]
    return pl.pallas_call(
        pack_kernel,
        in_specs=[SMEM] + [pl.BlockSpec(memory_space=pltpu.VMEM)] * len(operands),
        out_specs=[pl.BlockSpec(memory_space=pltpu.VMEM)] * 2,
        out_shape=[shape_of(FIRST_ROWS, D, BF16), shape_of(SECOND_ROWS, D, BF16)],
        cost_estimate=cost(2),
        name="pack",
    )(place, *operands)


def across(values, bits):
    return lax.ppermute(values, "fsdp", [(i, i ^ bits) for i in range(8)])


def along(values, step):
    return lax.ppermute(values, "dp", [(i, (i + step) % 4) for i in range(4)])


def gather_rows(packed):
    return jnp.stack([packed] + [along(packed, step) for step in (1, 2, 3)])


def shares_along(blocks):
    return [blocks[0]] + [along(blocks[step], step) for step in (1, 2, 3)]


def added(parts):
    return sum(part.astype(F32) for part in parts)


def spread(vector, index, devices):
    share = vector.shape[0]
    full = jnp.tile(vector, devices)
    mine = lax.broadcasted_iota(jnp.int32, full.shape, 0) // share == index
    return jnp.where(mine, full, jnp.zeros_like(full)).reshape(-1, D)


def finish_kernel(place, *refs):
    first, second, outs = refs[:4], refs[4:8], refs[8:]
    query, key, value, out, up, down, bias_up, bias_down, *norms = outs

    def summed(parts, rows):
        return sum(part[rows, :].astype(F32) for part in parts)

    for place_of, ref in enumerate((query, key, value)):
        ref[...] = summed(first, slice(place_of * SHARE, place_of * SHARE + SHARE))
    out[...] = summed(second, slice(0, SHARE))
    up[...] = summed(second, slice(SHARE, 5 * SHARE))
    for part in range(4):
        at = (5 + part) * SHARE
        down[:, D * part : D * part + D] = summed(second, slice(at, at + SHARE))
    device = place[0] * 8 + place[1]
    shift = lax.rem(D - device * SHARE, D)
    mine_first = pltpu.roll(summed(first, slice(3 * SHARE, FIRST_ROWS)), shift, 1)
    vectors = summed(second, slice(9 * SHARE, SECOND_ROWS))
    mine_second = pltpu.roll(vectors, shift, 1)
    row = lax.broadcasted_iota(jnp.int32, (8, D), 0)
    wide = jnp.sum(jnp.where(row == 3 + device // 8, vectors, 0.0), axis=0, keepdims=True)
    wide = pltpu.roll(jnp.broadcast_to(wide, (8, D)), lax.rem(D - (device % 8) * 4 * SHARE, D), 1)
    bias_up[...] = wide[0:1, : 4 * SHARE]
    bias_down[...] = mine_second[2:3, :SHARE]
    gain_attn, shift_attn, gain_ffn, shift_ffn = norms
    gain_attn[...] = mine_first[0:1, :SHARE]
    shift_attn[...] = mine_first[1:2, :SHARE]
    gain_ffn[...] = mine_second[0:1, :SHARE]
    shift_ffn[...] = mine_second[1:2, :SHARE]


def finish(place, first, second):
    shapes = [(SHARE, D)] * 4 + [(4 * SHARE, D), (SHARE, FF), (1, 4 * SHARE)] + [(1, SHARE)] * 5
    grads = pl.pallas_call(
        finish_kernel,
        in_specs=[SMEM] + [pl.BlockSpec(memory_space=pltpu.VMEM)] * 8,
        out_specs=[pl.BlockSpec(memory_space=pltpu.VMEM)] * 12,
        out_shape=[shape_of(rows, columns, F32) for rows, columns in shapes],
        cost_estimate=cost(2),
        name="finish",
    )(place, *first, *second)
    return [grad.T for grad in grads[:6]] + [grad.reshape(-1) for grad in grads[6:]]


def exchange_permutes(place, tokens, lengths, weights, vectors, cotangent):
    first, second = pack(place, weights, vectors)
    rows = gather_rows(first)
    in_x, in_y = across(rows, 2), across(rows, 4)
    diagonal = jnp.concatenate([across(in_x[:2], 4), across(in_y[2:], 2)])
    near = jnp.concatenate([rows, in_x, in_y, diagonal])
    second_rows = gather_rows(second)
    near, second_rows = lax.optimization_barrier((near, second_rows))
    first_blocks = (near, across(near, 1))
    first_blocks, second_rows = lax.optimization_barrier((first_blocks, second_rows))
    others = [across(second_rows, bits) for bits in (2, 4, 6)]
    *kept, attn, total, weights, gains = attend(lengths, place, False, tokens, first_blocks)
    kept += [weights, gains]
    attn, total, others = lax.optimization_barrier((attn, total, others))
    near = jnp.concatenate([second_rows] + others)
    second_blocks = (near, across(near, 1))
    output, middle_grad, numer_grad, total_grad, *parts = feed(
        place, False, tokens, attn, total, cotangent, second_blocks
    )
    others = [across(parts[chip], bits) for chip, bits in ((1, 2), (2, 4), (3, 6))]
    grad_tokens, near, far = attend_back(
        lengths, place, False, tokens, middle_grad, numer_grad, total_grad, kept
    )
    near, far, others = lax.optimization_barrier((near, far, others))
    second = added([parts[0]] + others).astype(BF16)
    second = added([second[:4], across(second[4:], 1)]).astype(BF16)
    first = added([near, across(far, 1)]).astype(BF16).reshape(4, 4, FIRST_ROWS, D)
    by_x, by_y = first[:, :2], first[:, 2:]
    sent_x = across(jnp.stack([by_x[1], by_x[3]]), 2)
    sent_y = across(jnp.stack([by_y[2], by_y[3]]), 4)
    by_x = added([jnp.stack([by_x[0], by_x[2]]), sent_x]).astype(BF16)
    by_y = added([jnp.stack([by_y[0], by_y[1]]), sent_y]).astype(BF16)
    by_x = added([by_x[0], across(by_x[1], 4)]).astype(BF16)
    by_y = added([by_y[0], across(by_y[1], 2)]).astype(BF16)
    first = shares_along([by_x[0], by_x[1], by_y[0], by_y[1]])
    second = shares_along(second)
    return output, grad_tokens, finish(place, first, second)


def exchange_plain(index, devices, tokens, lengths, weights, vectors, cotangent):
    w_query, w_key, w_value, w_out, w_up, w_down = weights
    bias_up, bias_down, gain_attn, shift_attn, gain_ffn, shift_ffn = vectors
    share = D // devices

    def gathered(rows):
        return lax.all_gather(rows, AXES, axis=0, tiled=True).reshape(32, SHARE, D)

    def vector_rows(parts):
        rows = jnp.concatenate([spread(part, index, devices) for part in parts])
        rows = lax.psum(rows, AXES)
        pad = jnp.zeros((8 - rows.shape[0], D), rows.dtype)
        rows = jnp.concatenate([rows, pad])[None]
        return jnp.concatenate([rows, jnp.zeros((31, 8, D), rows.dtype)])

    def halved(parts):
        blocks = jnp.concatenate(parts, axis=1)
        return blocks[:16], blocks[16:]

    place = jnp.zeros((2,), jnp.int32)
    first_blocks = halved(
        [gathered(w.T) for w in (w_query, w_key, w_value)]
        + [vector_rows([gain_attn, shift_attn])]
    )
    up = lax.all_gather(w_up.T, AXES, axis=0, tiled=True).reshape(32, 4 * SHARE, D)
    down = lax.all_gather(w_down.T, AXES, axis=0, tiled=True).reshape(32, SHARE, 4, D)
    down = jnp.transpose(down, (0, 2, 1, 3)).reshape(32, 4 * SHARE, D)
    second_blocks = halved(
        [gathered(w_out.T), up, down, vector_rows([gain_ffn, shift_ffn, bias_down, bias_up])]
    )
    *kept, attn, total, weights, gains = attend(lengths, place, True, tokens, first_blocks)
    kept += [weights, gains]
    output, middle_grad, numer_grad, total_grad, *parts = feed(
        place, True, tokens, attn, total, cotangent, second_blocks
    )
    second = jnp.stack(parts).reshape(4, 2, 4, SECOND_ROWS, D)
    second = jnp.transpose(second, (1, 0, 2, 3, 4)).reshape(32, SECOND_ROWS, D)
    grad_tokens, near, far = attend_back(
        lengths, place, True, tokens, middle_grad, numer_grad, total_grad, kept
    )
    first = jnp.concatenate([near, far])

    def scattered(rows):
        rows = rows.reshape(devices, -1, D)
        return lax.psum_scatter(rows, AXES, scatter_dimension=0, tiled=False).astype(F32)

    down = second[:, 5 * SHARE : 9 * SHARE].reshape(32, 4, SHARE, D)
    down = scattered(jnp.transpose(down, (0, 2, 1, 3)).reshape(32, 4 * SHARE, D))
    down = jnp.transpose(down.reshape(share, 4, D), (1, 0, 2)).reshape(4 * share, D)
    first_vectors = lax.psum(first[0, 3 * SHARE :].astype(F32), AXES)
    second_vectors = lax.psum(second[0, 9 * SHARE :].astype(F32), AXES)
    down = jnp.transpose(down.reshape(4, share, D), (0, 2, 1)).reshape(FF, share)

    def own(row):
        return lax.dynamic_slice(row, (index * share,), (share,))

    return (
        output,
        grad_tokens,
        [
            *[scattered(first[:, p * SHARE : p * SHARE + SHARE]).T for p in range(3)],
            scattered(second[:, :SHARE]).T,
            scattered(second[:, SHARE : 5 * SHARE]).T,
            down,
            lax.dynamic_slice(second_vectors[3:7].reshape(FF), (index * 4 * share,), (4 * share,)),
            own(second_vectors[2]),
            own(first_vectors[0]),
            own(first_vectors[1]),
            own(second_vectors[0]),
            own(second_vectors[1]),
        ],
    )


def on_device(sizes, tokens, lengths, *rest):
    weights, vectors, cotangent = rest[:6], rest[6:12], rest[12]
    if sizes == (4, 8):
        place = jnp.stack([lax.axis_index("dp"), lax.axis_index("fsdp")]).astype(jnp.int32)
        output, grad_tokens, grads = exchange_permutes(
            place, tokens, lengths, weights, vectors, cotangent
        )
    else:
        index = lax.axis_index(AXES)
        output, grad_tokens, grads = exchange_plain(
            index, sizes[0] * sizes[1], tokens, lengths, weights, vectors, cotangent
        )
    return (output, grad_tokens, *grads)


def solution(mesh):
    rows = P(AXES, None)
    columns = P(None, AXES)
    vector = P(AXES)
    sizes = (mesh.shape["dp"], mesh.shape["fsdp"])
    return jax.shard_map(
        functools.partial(on_device, sizes),
        mesh=mesh,
        in_specs=(rows, vector) + (columns,) * 6 + (vector,) * 6 + (rows,),
        out_specs=(rows, rows) + (columns,) * 6 + (vector,) * 6,
        check_vma=False,
    )
```

profile of v0, /device:TPU:0, one launch (start us, length us, event | category | flops | bytes accessed | tf_op | source)
XLA Modules:
  0.0 241.7 jit_solution(17174341246986030700)
XLA Ops:
  0.6 0.7 pad_add_fusion.place
  1.3 1.8 pack.1
  3.1 5.0 %collective-permute-start.2 = (bf16[56,512]{1,0:T(8,128)(2,1)}, bf16[56,512]{1,0:T(8,128)(2,1)S(1)}, u32[]{:S(2)}, u32[]{:S(2)}) collective-permute-start(bf16[56,512]{1,0:T(8,128)(2,1)} %get-tuple-element.62), channel_id=1, source_target_pairs={{0,24},{8,0},{16,8},{24,16},{1,25},{9,1},{17,9},{25,17},{2,26},{10... | collective-permute-start | bytes 172040 | tf_op jit(solution)/shard_map/ppermute | solution.py:792
  8.2 1.0 collective-permute-start
  9.2 2.8 %collective-permute-start.9 = (bf16[152,512]{1,0:T(8,128)(2,1)}, bf16[152,512]{1,0:T(8,128)(2,1)S(1)}, u32[]{:S(2)}, u32[]{:S(2)}) collective-permute-start(bf16[152,512]{1,0:T(8,128)(2,1)} %get-tuple-element.63), channel_id=1, source_target_pairs={{0,24},{8,0},{16,8},{24,16},{1,25},{9,1},{17,9},{25,17},{2,26},{10... | collective-permute-start | bytes 466952 | tf_op jit(solution)/shard_map/ppermute | solution.py:792
  12.0 1.1 collective-permute-start.8
  13.1 0.8 constant_dynamic-update-slice_fusion.7
  13.9 0.0 collective-permute-done.2
  13.9 0.0 collective-permute-start.7
  14.0 0.6 collective-permute-done.1
  14.6 0.5 collective-permute-done
  15.0 0.8 pad_maximum_fusion.1
  15.9 1.6 collective-permute-start.4
  17.5 1.5 collective-permute-start.3
  19.0 8.5 %collective-permute-done.8 = bf16[152,512]{1,0:T(8,128)(2,1)S(1)} collective-permute-done((bf16[152,512]{1,0:T(8,128)(2,1)}, bf16[152,512]{1,0:T(8,128)(2,1)S(1)}, u32[]{:S(2)}, u32[]{:S(2)}) %collective-permute-start.8) | collective-permute-done | bytes 155680 | tf_op jit(solution)/shard_map/ppermute | solution.py:792
  27.5 1.0 pad_maximum_fusion
  28.5 0.0 collective-permute-done.4
  28.6 1.6 collective-permute-start.6
  30.1 1.6 collective-permute-start.5
  31.8 3.2 %collective-permute-done.5 = bf16[2,56,512]{2,1,0:T(8,128)(2,1)S(1)} collective-permute-done((bf16[2,56,512]{2,1,0:T(8,128)(2,1)S(1)}, bf16[2,56,512]{2,1,0:T(8,128)(2,1)S(1)}, u32[]{:S(2)}, u32[]{:S(2)}) %collective-permute-start.5) | collective-permute-done | bytes 114720 | tf_op jit(solution)/shard_map/ppermute | solution.py:788
  35.0 0.0 copy-start.2
  35.0 0.1 collective-permute-start.10
  35.1 2.5 %collective-permute-done.10.far_blocks = bf16[16,56,512]{2,1,0:T(8,128)(2,1)S(1)} collective-permute-done((bf16[16,56,512]{2,1,0:T(8,128)(2,1)S(1)}, bf16[16,56,512]{2,1,0:T(8,128)(2,1)S(1)}, u32[]{:S(2)}, u32[]{:S(2)}) %collective-permute-start.10) | collective-permute-done | bytes 917536 | tf_op jit(solution)/shard_map/ppermute | solution.py:788
  37.6 1.5 collective-permute-start.13
  39.1 0.5 collective-permute-start.12
  39.6 1.5 collective-permute-start.11
  41.1 34.0 %attend.1 = (bf16[6576,512]{1,0:T(8,128)(2,1)}, bf16[6576,512]{1,0:T(8,128)(2,1)}, bf16[6576,512]{1,0:T(8,128)(2,1)}, bf16[12288,512]{1,0:T(8,128)(2,1)}, bf16[3...) custom-call(s32[3]{0:T(128)} %lengths.3, s32[2]{0:T(128)} %pad_add_fusion.place, ...), custom_call_target="tpu_custom_call" | custom-call | flops 40000000000 | bytes 40000000 | tf_op jit(solution)/shard_map/attend/pallas_call | solution.py:619
  75.1 1.1 constant_dynamic-update-slice_fusion.10
  76.3 1.1 constant_dynamic-update-slice_fusion.9
  77.4 1.1 constant_dynamic-update-slice_fusion.8.near_blocks
  78.5 1.4 copy-done.1
  80.0 4.9 %collective-permute-done.14.far_blocks = bf16[16,152,512]{2,1,0:T(8,128)(2,1)} collective-permute-done((bf16[16,152,512]{2,1,0:T(8,128)(2,1)S(1)}, bf16[16,152,512]{2,1,0:T(8,128)(2,1)}, u32[]{:S(2)}, u32[]{:S(2)}) %collective-permute-start.14) | collective-permute-done | bytes 2490400 | tf_op jit(solution)/shard_map/ppermute | solution.py:788
  84.8 65.7 %feed.1 = (bf16[3072,512]{1,0:T(8,128)(2,1)}, bf16[3072,512]{1,0:T(8,128)(2,1)}, bf16[3072,512]{1,0:T(8,128)(2,1)}, bf16[3072,512]{1,0:T(8,128)(2,1)}, bf16[8,15...) custom-call(s32[2]{0:T(128)} %pad_add_fusion.place, ...), custom_call_target="tpu_custom_call" | custom-call | flops 74999996416 | bytes 75000000 | tf_op jit(solution)/shard_map/feed/pallas_call | solution.py:669
  150.5 0.6 collective-permute-start.15
  151.1 1.5 collective-permute-start.16
  152.6 1.4 collective-permute-start.17
  154.0 49.9 %attend_back.1 = (bf16[3072,512]{1,0:T(8,128)(2,1)}, bf16[16,56,512]{2,1,0:T(8,128)(2,1)}, bf16[16,56,512]{2,1,0:T(8,128)(2,1)}) custom-call(s32[3]{0:T(128)} %lengths.3, s32[2]{0:T(128)} %pad_add_fusion.place, bf16[3072,512]{1,0:T(8,128)(2,1)} %tokens.5, bf16[3072,512]{1,0:T(8,128)(2,1)} %get-tuple-element.77.middle_grad, ...), custom_call_target="tpu_custom_call" | custom-call | flops 60000002048 | bytes 60000000 | tf_op jit(solution)/shard_map/attend_back/pallas_call | solution.py:706
  204.0 2.3 collective-permute-done.16
  206.3 1.6 collective-permute-done.17
  207.9 3.2 %add_convert_fusion = bf16[8,152,512]{2,1,0:T(8,128)(2,1)S(1)} fusion(bf16[8,152,512]{2,1,0:T(8,128)(2,1)} %collective-permute-done.17, bf16[8,152,512]{2,1,0:T(8,128)(2,1)} %collective-permute-done.16, bf16[8,152,512]{2,1,0:T(8,128)(2,1)} %collective-permute-done.15, bf16[8,152,512]{2,1,0:T(8,128)(2,1)} %get-tuple-element.94), kind=kLoop, calls=%fused_computation | loop fusion | flops 4980736 | bytes 6225920 | tf_op jit(solution)/shard_map/convert_element_type | solution.py:882
  211.1 0.1 collective-permute-start.26
  211.2 0.5 collective-permute-start.18
  211.7 1.5 collective-permute-done.26
  213.2 0.2 add_convert_fusion.2
  213.4 0.7 slice_bitcast_fusion
  214.1 1.8 collective-permute-start.28
  215.9 2.0 collective-permute-start.27
  217.9 0.3 add_convert_fusion.1
  218.2 0.9 collective-permute-start.22
  219.2 1.5 collective-permute-start.19
  220.8 4.4 %collective-permute-done.22 = bf16[2,2,56,512]{3,2,1,0:T(8,128)(2,1)S(1)} collective-permute-done((bf16[2,2,56,512]{3,2,1,0:T(8,128)(2,1)S(1)}, bf16[2,2,56,512]{3,2,1,0:T(8,128)(2,1)S(1)}, u32[]{:S(2)}, u32[]{:S(2)}) %collective-permute-start.22) | collective-permute-done | bytes 229408 | tf_op jit(solution)/shard_map/ppermute | solution.py:788
  225.1 0.1 add_convert_fusion.3
  225.2 0.9 collective-permute-start.23
  226.1 0.1 add_convert_fusion.4
  226.2 1.6 collective-permute-start.20
  227.7 2.3 collective-permute-done.23
  230.1 2.1 collective-permute-start.25
  232.3 0.6 slice_bitcast_fusion.10
  232.9 1.4 collective-permute-start.21
  234.3 0.0 collective-permute-done.25.refs_3_
  234.4 2.9 %collective-permute-done.24.refs_2_ = bf16[56,512]{1,0:T(8,128)(2,1)S(1)} collective-permute-done((bf16[56,512]{1,0:T(8,128)(2,1)S(1)}, bf16[56,512]{1,0:T(8,128)(2,1)S(1)}, u32[]{:S(2)}, u32[]{:S(2)}) %collective-permute-start.24) | collective-permute-done | bytes 57376 | tf_op jit(solution)/shard_map/ppermute | solution.py:792
  237.3 1.6 collective-permute-done.21.refs_1_
  238.9 0.6 copy-done.10
  239.5 2.0 finish.1
  (56 shorter events, 0.4 us)
Async XLA Ops:
  3.1 10.8 %collective-permute-start.2 = (bf16[56,512]{1,0:T(8,128)(2,1)}, bf16[56,512]{1,0:T(8,128)(2,1)S(1)}, u32[]{:S(2)}, u32[]{:S(2)}) collective-permute-start(bf16[56,512]{1,0:T(8,128)(2,1)} %get-tuple-element.62), channel_id=1, source_target_pairs={{0,24},{8,0},{16,8},{24,16},{1,25},{9,1},{17,9},{25,17},{2,26},{10... | collective-permute-start | bytes 172040 | tf_op jit(solution)/shard_map/ppermute | solution.py:792
  8.2 6.4 %collective-permute-start.1 = (bf16[56,512]{1,0:T(8,128)(2,1)}, bf16[56,512]{1,0:T(8,128)(2,1)S(1)}, u32[]{:S(2)}, u32[]{:S(2)}) collective-permute-start(bf16[56,512]{1,0:T(8,128)(2,1)} %get-tuple-element.62), channel_id=1, source_target_pairs={{0,16},{8,24},{16,0},{24,8},{1,17},{9,25},{17,1},{25,9},{2,18},{10... | collective-permute-start | bytes 172040 | tf_op jit(solution)/shard_map/ppermute | solution.py:792
  8.2 6.9 %collective-permute-start = (bf16[56,512]{1,0:T(8,128)(2,1)}, bf16[56,512]{1,0:T(8,128)(2,1)S(1)}, u32[]{:S(2)}, u32[]{:S(2)}) collective-permute-start(bf16[56,512]{1,0:T(8,128)(2,1)} %get-tuple-element.62), channel_id=1, source_target_pairs={{0,8},{8,16},{16,24},{24,0},{1,9},{9,17},{17,25},{25,1},{2,10},{10... | collective-permute-start | bytes 172040 | tf_op jit(solution)/shard_map/ppermute | solution.py:792
  9.2 9.8 %collective-permute-start.9 = (bf16[152,512]{1,0:T(8,128)(2,1)}, bf16[152,512]{1,0:T(8,128)(2,1)S(1)}, u32[]{:S(2)}, u32[]{:S(2)}) collective-permute-start(bf16[152,512]{1,0:T(8,128)(2,1)} %get-tuple-element.63), channel_id=1, source_target_pairs={{0,24},{8,0},{16,8},{24,16},{1,25},{9,1},{17,9},{25,17},{2,26},{10... | collective-permute-start | bytes 466952 | tf_op jit(solution)/shard_map/ppermute | solution.py:792
  12.0 15.5 %collective-permute-start.8 = (bf16[152,512]{1,0:T(8,128)(2,1)}, bf16[152,512]{1,0:T(8,128)(2,1)S(1)}, u32[]{:S(2)}, u32[]{:S(2)}) collective-permute-start(bf16[152,512]{1,0:T(8,128)(2,1)} %get-tuple-element.63), channel_id=1, source_target_pairs={{0,16},{8,24},{16,0},{24,8},{1,17},{9,25},{17,1},{25,9},{2,18},{10... | collective-permute-start | bytes 466952 | tf_op jit(solution)/shard_map/ppermute | solution.py:792
  13.9 13.6 %collective-permute-start.7 = (bf16[152,512]{1,0:T(8,128)(2,1)}, bf16[152,512]{1,0:T(8,128)(2,1)S(1)}, u32[]{:S(2)}, u32[]{:S(2)}) collective-permute-start(bf16[152,512]{1,0:T(8,128)(2,1)} %get-tuple-element.63), channel_id=1, source_target_pairs={{0,8},{8,16},{16,24},{24,0},{1,9},{9,17},{17,25},{25,1},{2,10},{10... | collective-permute-start | bytes 466952 | tf_op jit(solution)/shard_map/ppermute | solution.py:792
  15.9 12.7 %collective-permute-start.4 = (bf16[4,56,512]{2,1,0:T(8,128)(2,1)S(1)}, bf16[4,56,512]{2,1,0:T(8,128)(2,1)S(1)}, u32[]{:S(2)}, u32[]{:S(2)}) collective-permute-start(bf16[4,56,512]{2,1,0:T(8,128)(2,1)S(1)} %pad_maximum_fusion.1), channel_id=1, source_target_pairs={{0,4},{1,5},{2,6},{3,7},{4,0},{5,1},{6,2},{7,3},{8,12},{9,13},{10,... | collective-permute-start | bytes 688136 | tf_op jit(solution)/shard_map/ppermute | solution.py:788
  17.5 12.7 %collective-permute-start.3 = (bf16[4,56,512]{2,1,0:T(8,128)(2,1)S(1)}, bf16[4,56,512]{2,1,0:T(8,128)(2,1)S(1)}, u32[]{:S(2)}, u32[]{:S(2)}) collective-permute-start(bf16[4,56,512]{2,1,0:T(8,128)(2,1)S(1)} %pad_maximum_fusion.1), channel_id=1, source_target_pairs={{0,2},{1,3},{2,0},{3,1},{4,6},{5,7},{6,4},{7,5},{8,10},{9,11},{10,... | collective-permute-start | bytes 688136 | tf_op jit(solution)/shard_map/ppermute | solution.py:788
  28.6 6.4 %collective-permute-start.6 = (bf16[2,56,512]{2,1,0:T(8,128)(2,1)S(1)}, bf16[2,56,512]{2,1,0:T(8,128)(2,1)S(1)}, u32[]{:S(2)}, u32[]{:S(2)}) collective-permute-start(bf16[2,56,512]{2,1,0:T(8,128)(2,1)S(1)} %slice.97), channel_id=1, source_target_pairs={{0,2},{1,3},{2,0},{3,1},{4,6},{5,7},{6,4},{7,5},{8,10},{9,11},{10,... | collective-permute-start | bytes 344072 | tf_op jit(solution)/shard_map/ppermute | solution.py:788
  30.1 4.9 %collective-permute-start.5 = (bf16[2,56,512]{2,1,0:T(8,128)(2,1)S(1)}, bf16[2,56,512]{2,1,0:T(8,128)(2,1)S(1)}, u32[]{:S(2)}, u32[]{:S(2)}) collective-permute-start(bf16[2,56,512]{2,1,0:T(8,128)(2,1)S(1)} %slice.96), channel_id=1, source_target_pairs={{0,4},{1,5},{2,6},{3,7},{4,0},{5,1},{6,2},{7,3},{8,12},{9,13},{10,... | collective-permute-start | bytes 344072 | tf_op jit(solution)/shard_map/ppermute | solution.py:788
  35.0 4.0 %copy-start.2 = (bf16[16,56,512]{2,1,0:T(8,128)(2,1)}, bf16[16,56,512]{2,1,0:T(8,128)(2,1)S(1)}, u32[]{:S(2)}) copy-start(bf16[16,56,512]{2,1,0:T(8,128)(2,1)S(1)} %constant_dynamic-update-slice_fusion.near_blocks) | copy-start | bytes 2752516
  35.0 2.5 %collective-permute-start.10 = (bf16[16,56,512]{2,1,0:T(8,128)(2,1)S(1)}, bf16[16,56,512]{2,1,0:T(8,128)(2,1)S(1)}, u32[]{:S(2)}, u32[]{:S(2)}) collective-permute-start(bf16[16,56,512]{2,1,0:T(8,128)(2,1)S(1)} %constant_dynamic-update-slice_fusion.near_blocks), channel_id=1, source_target_pairs={{0,1},{1,0},{2,3},{3,2},{4,5},{5,4},{6,7},{7,6},{8,9},{9,8},{10,11... | collective-permute-start | bytes 2752520 | tf_op jit(solution)/shard_map/ppermute | solution.py:788
  37.6 2.0 copy-start.4
  37.6 37.5 %collective-permute-start.13 = (bf16[4,152,512]{2,1,0:T(8,128)(2,1)S(1)}, bf16[4,152,512]{2,1,0:T(8,128)(2,1)}, u32[]{:S(2)}, u32[]{:S(2)}) collective-permute-start(bf16[4,152,512]{2,1,0:T(8,128)(2,1)S(1)} %pad_maximum_fusion), channel_id=1, source_target_pairs={{0,6},{1,7},{2,4},{3,5},{4,2},{5,3},{6,0},{7,1},{8,14},{9,15},{10,... | collective-permute-start | bytes 1867784 | tf_op jit(solution)/shard_map/ppermute | solution.py:788
  39.1 36.1 %collective-permute-start.12 = (bf16[4,152,512]{2,1,0:T(8,128)(2,1)S(1)}, bf16[4,152,512]{2,1,0:T(8,128)(2,1)}, u32[]{:S(2)}, u32[]{:S(2)}) collective-permute-start(bf16[4,152,512]{2,1,0:T(8,128)(2,1)S(1)} %pad_maximum_fusion), channel_id=1, source_target_pairs={{0,4},{1,5},{2,6},{3,7},{4,0},{5,1},{6,2},{7,3},{8,12},{9,13},{10,... | collective-permute-start | bytes 1867784 | tf_op jit(solution)/shard_map/ppermute | solution.py:788
  39.6 35.6 %collective-permute-start.11 = (bf16[4,152,512]{2,1,0:T(8,128)(2,1)S(1)}, bf16[4,152,512]{2,1,0:T(8,128)(2,1)}, u32[]{:S(2)}, u32[]{:S(2)}) collective-permute-start(bf16[4,152,512]{2,1,0:T(8,128)(2,1)S(1)} %pad_maximum_fusion), channel_id=1, source_target_pairs={{0,2},{1,3},{2,0},{3,1},{4,6},{5,7},{6,4},{7,5},{8,10},{9,11},{10,... | collective-permute-start | bytes 1867784 | tf_op jit(solution)/shard_map/ppermute | solution.py:788
  78.5 1.4 copy-start.1
  80.0 4.9 %collective-permute-start.14 = (bf16[16,152,512]{2,1,0:T(8,128)(2,1)S(1)}, bf16[16,152,512]{2,1,0:T(8,128)(2,1)}, u32[]{:S(2)}, u32[]{:S(2)}) collective-permute-start(bf16[16,152,512]{2,1,0:T(8,128)(2,1)S(1)} %constant_dynamic-update-slice_fusion.8.near_blocks), channel_id=1, source_target_pairs={{0,1},{1,0},{2,3},{3,2},{4,5},{5,4},{6,7},{7,6},{8,9},{9,8},{10,11... | collective-permute-start | bytes 7471112 | tf_op jit(solution)/shard_map/ppermute | solution.py:788
  150.5 53.5 %collective-permute-start.15 = (bf16[8,152,512]{2,1,0:T(8,128)(2,1)}, bf16[8,152,512]{2,1,0:T(8,128)(2,1)}, u32[]{:S(2)}, u32[]{:S(2)}) collective-permute-start(bf16[8,152,512]{2,1,0:T(8,128)(2,1)} %get-tuple-element.89), channel_id=1, source_target_pairs={{0,2},{1,3},{2,0},{3,1},{4,6},{5,7},{6,4},{7,5},{8,10},{9,11},{10,... | collective-permute-start | bytes 3735560 | tf_op jit(solution)/shard_map/ppermute | solution.py:788
  151.1 55.2 %collective-permute-start.16 = (bf16[8,152,512]{2,1,0:T(8,128)(2,1)}, bf16[8,152,512]{2,1,0:T(8,128)(2,1)}, u32[]{:S(2)}, u32[]{:S(2)}) collective-permute-start(bf16[8,152,512]{2,1,0:T(8,128)(2,1)} %get-tuple-element.90), channel_id=1, source_target_pairs={{0,4},{1,5},{2,6},{3,7},{4,0},{5,1},{6,2},{7,3},{8,12},{9,13},{10,... | collective-permute-start | bytes 3735560 | tf_op jit(solution)/shard_map/ppermute | solution.py:788
  152.6 55.3 %collective-permute-start.17 = (bf16[8,152,512]{2,1,0:T(8,128)(2,1)}, bf16[8,152,512]{2,1,0:T(8,128)(2,1)}, u32[]{:S(2)}, u32[]{:S(2)}) collective-permute-start(bf16[8,152,512]{2,1,0:T(8,128)(2,1)} %get-tuple-element.91), channel_id=1, source_target_pairs={{0,6},{1,7},{2,4},{3,5},{4,2},{5,3},{6,0},{7,1},{8,14},{9,15},{10,... | collective-permute-start | bytes 3735560 | tf_op jit(solution)/shard_map/ppermute | solution.py:788
  207.9 3.3 %copy-start.3 = (bf16[16,56,512]{2,1,0:T(8,128)(2,1)S(1)}, bf16[16,56,512]{2,1,0:T(8,128)(2,1)}, u32[]{:S(2)}) copy-start(bf16[16,56,512]{2,1,0:T(8,128)(2,1)} %get-tuple-element.93) | copy-start | bytes 2752516
  211.0 6.9 %copy-start = (bf16[16,56,512]{2,1,0:T(8,128)(2,1)S(1)}, bf16[16,56,512]{2,1,0:T(8,128)(2,1)}, u32[]{:S(2)}) copy-start(bf16[16,56,512]{2,1,0:T(8,128)(2,1)} %get-tuple-element.92) | copy-start | bytes 2752516
  211.1 2.1 collective-permute-start.26
  211.2 6.7 %collective-permute-start.18 = (bf16[16,56,512]{2,1,0:T(8,128)(2,1)S(1)}, bf16[16,56,512]{2,1,0:T(8,128)(2,1)S(1)}, u32[]{:S(2)}, u32[]{:S(2)}) collective-permute-start(bf16[16,56,512]{2,1,0:T(8,128)(2,1)S(1)} %copy-done.3), channel_id=1, source_target_pairs={{0,1},{1,0},{2,3},{3,2},{4,5},{5,4},{6,7},{7,6},{8,9},{9,8},{10,11... | collective-permute-start | bytes 2752520 | tf_op jit(solution)/shard_map/ppermute | solution.py:788
  214.1 18.8 %collective-permute-start.29 = (bf16[152,512]{1,0:T(8,128)(2,1)S(1)}, bf16[152,512]{1,0:T(8,128)(2,1)S(1)}, u32[]{:S(2)}, u32[]{:S(2)}) collective-permute-start(bf16[152,512]{1,0:T(8,128)(2,1)S(1)} %get-tuple-element.114), channel_id=1, source_target_pairs={{0,24},{8,0},{16,8},{24,16},{1,25},{9,1},{17,9},{25,17},{2,26},{10... | collective-permute-start | bytes 466952 | tf_op jit(solution)/shard_map/ppermute | solution.py:792
  214.1 20.2 %collective-permute-start.28 = (bf16[152,512]{1,0:T(8,128)(2,1)S(1)}, bf16[152,512]{1,0:T(8,128)(2,1)S(1)}, u32[]{:S(2)}, u32[]{:S(2)}) collective-permute-start(bf16[152,512]{1,0:T(8,128)(2,1)S(1)} %get-tuple-element.115), channel_id=1, source_target_pairs={{0,16},{8,24},{16,0},{24,8},{1,17},{9,25},{17,1},{25,9},{2,18},{10... | collective-permute-start | bytes 466952 | tf_op jit(solution)/shard_map/ppermute | solution.py:792
  215.9 18.4 %collective-permute-start.27 = (bf16[152,512]{1,0:T(8,128)(2,1)S(1)}, bf16[152,512]{1,0:T(8,128)(2,1)S(1)}, u32[]{:S(2)}, u32[]{:S(2)}) collective-permute-start(bf16[152,512]{1,0:T(8,128)(2,1)S(1)} %get-tuple-element.116), channel_id=1, source_target_pairs={{0,8},{8,16},{16,24},{24,0},{1,9},{9,17},{17,25},{25,1},{2,10},{10... | collective-permute-start | bytes 466952 | tf_op jit(solution)/shard_map/ppermute | solution.py:792
  218.2 6.9 %collective-permute-start.22 = (bf16[2,2,56,512]{3,2,1,0:T(8,128)(2,1)S(1)}, bf16[2,2,56,512]{3,2,1,0:T(8,128)(2,1)S(1)}, u32[]{:S(2)}, u32[]{:S(2)}) collective-permute-start(bf16[2,2,56,512]{3,2,1,0:T(8,128)(2,1)S(1)} %stack.69), channel_id=1, source_target_pairs={{0,4},{1,5},{2,6},{3,7},{4,0},{5,1},{6,2},{7,3},{8,12},{9,13},{10,... | collective-permute-start | bytes 688136 | tf_op jit(solution)/shard_map/ppermute | solution.py:788
  219.2 6.9 %collective-permute-start.19 = (bf16[2,2,56,512]{3,2,1,0:T(8,128)(2,1)S(1)}, bf16[2,2,56,512]{3,2,1,0:T(8,128)(2,1)S(1)}, u32[]{:S(2)}, u32[]{:S(2)}) collective-permute-start(bf16[2,2,56,512]{3,2,1,0:T(8,128)(2,1)S(1)} %pad_maximum_fusion.2), channel_id=1, source_target_pairs={{0,2},{1,3},{2,0},{3,1},{4,6},{5,7},{6,4},{7,5},{8,10},{9,11},{10,... | collective-permute-start | bytes 688136 | tf_op jit(solution)/shard_map/ppermute | solution.py:788
  225.2 4.9 %collective-permute-start.23 = (bf16[2,56,512]{2,1,0:T(8,128)(2,1)S(1)}, bf16[2,56,512]{2,1,0:T(8,128)(2,1)S(1)}, u32[]{:S(2)}, u32[]{:S(2)}) collective-permute-start(bf16[2,56,512]{2,1,0:T(8,128)(2,1)S(1)} %slice_bitcast_fusion.4), channel_id=1, source_target_pairs={{0,2},{1,3},{2,0},{3,1},{4,6},{5,7},{6,4},{7,5},{8,10},{9,11},{10,... | collective-permute-start | bytes 344072 | tf_op jit(solution)/shard_map/ppermute | solution.py:788
  226.2 6.1 %collective-permute-start.20 = (bf16[2,56,512]{2,1,0:T(8,128)(2,1)S(1)}, bf16[2,56,512]{2,1,0:T(8,128)(2,1)S(1)}, u32[]{:S(2)}, u32[]{:S(2)}) collective-permute-start(bf16[2,56,512]{2,1,0:T(8,128)(2,1)S(1)} %slice_bitcast_fusion.6), channel_id=1, source_target_pairs={{0,4},{1,5},{2,6},{3,7},{4,0},{5,1},{6,2},{7,3},{8,12},{9,13},{10,... | collective-permute-start | bytes 344072 | tf_op jit(solution)/shard_map/ppermute | solution.py:788
  230.1 4.3 %collective-permute-start.25 = (bf16[56,512]{1,0:T(8,128)(2,1)S(1)}, bf16[56,512]{1,0:T(8,128)(2,1)S(1)}, u32[]{:S(2)}, u32[]{:S(2)}) collective-permute-start(bf16[56,512]{1,0:T(8,128)(2,1)S(1)} %get-tuple-element.118), channel_id=1, source_target_pairs={{0,24},{8,0},{16,8},{24,16},{1,25},{9,1},{17,9},{25,17},{2,26},{10... | collective-permute-start | bytes 172040 | tf_op jit(solution)/shard_map/ppermute | solution.py:792
  232.2 5.1 %collective-permute-start.24 = (bf16[56,512]{1,0:T(8,128)(2,1)S(1)}, bf16[56,512]{1,0:T(8,128)(2,1)S(1)}, u32[]{:S(2)}, u32[]{:S(2)}) collective-permute-start(bf16[56,512]{1,0:T(8,128)(2,1)S(1)} %get-tuple-element.119), channel_id=1, source_target_pairs={{0,16},{8,24},{16,0},{24,8},{1,17},{9,25},{17,1},{25,9},{2,18},{10... | collective-permute-start | bytes 172040 | tf_op jit(solution)/shard_map/ppermute | solution.py:792
  232.9 6.0 %copy-start.5 = (bf16[152,512]{1,0:T(8,128)(2,1)}, bf16[152,512]{1,0:T(8,128)(2,1)S(1)}, u32[]{:S(2)}) copy-start(bf16[152,512]{1,0:T(8,128)(2,1)S(1)} %collective-permute-done.29.refs_7_) | copy-start | bytes 466948
  232.9 6.0 %collective-permute-start.21 = (bf16[56,512]{1,0:T(8,128)(2,1)S(1)}, bf16[56,512]{1,0:T(8,128)(2,1)S(1)}, u32[]{:S(2)}, u32[]{:S(2)}) collective-permute-start(bf16[56,512]{1,0:T(8,128)(2,1)S(1)} %get-tuple-element.120), channel_id=1, source_target_pairs={{0,8},{8,16},{16,24},{24,0},{1,9},{9,17},{17,25},{25,1},{2,10},{10... | collective-permute-start | bytes 172040 | tf_op jit(solution)/shard_map/ppermute | solution.py:792
  234.3 4.6 %copy-start.6 = (bf16[152,512]{1,0:T(8,128)(2,1)}, bf16[152,512]{1,0:T(8,128)(2,1)S(1)}, u32[]{:S(2)}) copy-start(bf16[152,512]{1,0:T(8,128)(2,1)S(1)} %collective-permute-done.28.refs_6_) | copy-start | bytes 466948
  234.3 4.6 %copy-start.7 = (bf16[152,512]{1,0:T(8,128)(2,1)}, bf16[152,512]{1,0:T(8,128)(2,1)S(1)}, u32[]{:S(2)}) copy-start(bf16[152,512]{1,0:T(8,128)(2,1)S(1)} %collective-permute-done.27.refs_5_) | copy-start | bytes 466948
  234.4 4.5 %copy-start.8 = (bf16[56,512]{1,0:T(8,128)(2,1)}, bf16[56,512]{1,0:T(8,128)(2,1)S(1)}, u32[]{:S(2)}) copy-start(bf16[56,512]{1,0:T(8,128)(2,1)S(1)} %collective-permute-done.25.refs_3_) | copy-start | bytes 172036
  237.3 1.6 copy-start.9
  238.9 0.6 copy-start.10
where the time goes:
time: 242 us
  Pallas kernels  153 us (63%)
  waiting for transfers between devices  36.9 us (15%)
  starting transfers between devices  36.2 us (15%)
  local copies, waits for them, and re-layouts  7.81 us (3%)
  other arithmetic  6.29 us (3%)
    pallas_call x1, Pallas kernels, feed(): pl.pallas_call(functools.partial(feed_kernel, plain), grid=(rows // LEN,)...  65.7 us
    pallas_call x1, Pallas kernels, attend_back(): pl.pallas_call(functools.partial(attend_back_kernel, plain), grid=(count,...  49.9 us
    pallas_call x1, Pallas kernels, attend(): pl.pallas_call(functools.partial(attend_kernel, plain), grid=(count,), in...  34 us
    ppermute x18, waiting for transfers between devices, across(): return lax.ppermute(values, 'fsdp', [(i, i ^ bits) for i in range(8)])  22.7 us
    ppermute x18, starting transfers between devices, across(): return lax.ppermute(values, 'fsdp', [(i, i ^ bits) for i in range(8)])  18.8 us
    ppermute x12, starting transfers between devices, along(): return lax.ppermute(values, 'dp', [(i, (i + step) % 4) for i in range(4)])  17.4 us
    ppermute x12, waiting for transfers between devices, along(): return lax.ppermute(values, 'dp', [(i, (i + step) % 4) for i in range(4)])  14.2 us
    unnamed x32, local copies, waits for them, and re-layouts  5.21 us
  transfers between devices with their start and end apart: 30, of which 13 were waited for; matrix products, arithmetic and copies ran while one was open for 2% of the time, Pallas kernels for 35%

commit v1 on v0

--- a/solution.py
+++ b/solution.py
@@ -149,13 +149,13 @@
 def load_second(place, plain, blocks, w_out, w_up, w_down, vectors):
     total = jnp.zeros((8, D), F32)
     for half, block, device in block_places(place, plain, -1):
-        source = blocks[half]
-        w_out[sixteen(device), :] = source[block, 0:SHARE, :]
-        w_up[sixty_four(device), :] = source[block, SHARE : 5 * SHARE, :]
+        source = blocks[4 * half + block // 4].at[block % 4]
+        w_out[sixteen(device), :] = source[0:SHARE, :]
+        w_up[sixty_four(device), :] = source[SHARE : 5 * SHARE, :]
         for part in range(4):
             at = (5 + part) * SHARE
-            w_down[part, sixteen(device), :] = source[block, at : at + SHARE, :]
-        total = total + source[block, 9 * SHARE : 9 * SHARE + 8, :].astype(F32)
+            w_down[part, sixteen(device), :] = source[at : at + SHARE, :]
+        total = total + source[9 * SHARE : 9 * SHARE + 8, :].astype(F32)
     vectors[...] = total
 
 
@@ -207,21 +207,31 @@
     bias,
     pool,
     half,
+    query_out,
+    key_out,
+    value_out,
+    probs_out,
+    attn,
+    total,
+    weights,
+    vectors,
     query,
     key,
     value,
     probs,
-    attn,
-    total,
-    weights,
-    vectors,
     normed,
     joined,
     top,
     counts,
     numer,
     denom,
+    done,
 ):
+    def copy_out(index):
+        source = (query, key, value, probs)[index]
+        target = (query_out, key_out, value_out, probs_out)[index]
+        return pltpu.make_async_copy(source, target.at[pl.program_id(0)], done.at[index])
+
     @pl.when(pl.program_id(0) == 0)
     def _():
         load_first(place, plain, (near_blocks, far_blocks), weights, vectors)
@@ -265,6 +275,8 @@
                     top[chunk * count : chunk * count + count, lane : lane + D] = part
     for ref, lane in targets:
         ref[STARTS[-1] : STARTS[-1] + SIZES[-1], :] = top[:, lane : lane + D].astype(BF16)
+    for index in range(3):
+        copy_out(index).start()
 
     def score_step(rows, near, flat, kind):
         allowed = bias[kind]
@@ -274,6 +286,7 @@
             probs[flat, lanes] = jnp.exp2(scores * SCORE + allowed).astype(BF16)
 
     window_loop(score_step)
+    copy_out(3).start()
     low_head = lax.broadcasted_iota(jnp.int32, (QUERIES, 128), 1) < DH
 
     def value_step(rows, near, flat, kind):
@@ -298,50 +311,22 @@
             total[rows, lanes] = below
 
     row_loop(LEN, 64, join_step)
-
-
-def feed_kernel(
-    plain,
-    place,
-    tokens,
-    attn,
-    total,
-    cotangent,
-    near_blocks,
-    far_blocks,
-    output,
-    middle_grad,
-    numer_grad,
-    total_grad,
-    grads_0,
-    grads_1,
-    grads_2,
-    grads_3,
-    w_out,
-    w_up,
-    w_down,
-    vectors,
-    middle,
-    normed,
-    inverse,
-    normed_low,
-    hidden,
-    result,
-    gathered,
-    active,
-    back,
-    sums,
-    acc_out,
-    acc_up,
-    acc_down,
-):
+    for index in range(4):
+        copy_out(index).wait()
+
+
+def feed_kernel(plain, place, tokens, attn, total, cotangent, *refs):
+    blocks, (output, middle_grad, numer_grad, total_grad), grads = refs[:8], refs[8:12], refs[12:16]
+    w_out, w_up, w_down, vectors, middle, normed, inverse, normed_low = refs[16:24]
+    hidden, result, gathered, active, back, sums, acc_out, acc_up, acc_down = refs[24:]
+
     @pl.when(pl.program_id(0) == 0)
     def _():
         acc_out[...] = jnp.zeros_like(acc_out)
         acc_up[...] = jnp.zeros_like(acc_up)
         acc_down[...] = jnp.zeros_like(acc_down)
         sums[...] = jnp.zeros_like(sums)
-        load_second(place, plain, (near_blocks, far_blocks), w_out, w_up, w_down, vectors)
+        load_second(place, plain, blocks, w_out, w_up, w_down, vectors)
 
     gain = vectors[0:1, :]
     shift = vectors[1:2, :]
@@ -418,7 +403,7 @@
         small = jnp.sum(sums[...].reshape(7, 8, D), axis=1)
         small = jnp.concatenate([small, jnp.zeros((1, D), F32)], axis=0).astype(BF16)
         for half, block, device in block_places(place, plain, 1):
-            target = (grads_0, grads_1, grads_2, grads_3)[block // 4]
+            target = grads[block // 4]
             into = 4 * half + block % 4
             target[into, 0:SHARE, :] = acc_out[sixteen(device), :].astype(BF16)
             target[into, SHARE : 5 * SHARE, :] = acc_up[sixty_four(device), :].astype(BF16)
@@ -436,10 +421,10 @@
     middle_grad,
     numer_grad,
     total_grad,
-    query,
-    key,
-    value,
-    probs,
+    query_in,
+    key_in,
+    value_in,
+    probs_in,
     weights,
     vectors,
     pool,
@@ -457,12 +442,27 @@
     top,
     sums,
     acc,
+    query,
+    key,
+    value,
+    probs,
+    arrived,
 ):
     step_index = pl.program_id(0)
+    last = pl.num_programs(0) - 1
     length = lengths[step_index]
+
+    def copy_in(index, step):
+        source = (value_in, probs_in, key_in, query_in)[index]
+        target = (value, probs, key, query)[index]
+        return pltpu.make_async_copy(source.at[step], target, arrived.at[index])
+
+    following = jnp.minimum(step_index + 1, last)
 
     @pl.when(step_index == 0)
     def _():
+        for index in range(4):
+            copy_in(index, 0).start()
         acc[...] = jnp.zeros_like(acc)
         sums[...] = jnp.zeros_like(sums)
 
@@ -498,7 +498,11 @@
             right = jnp.concatenate([value[near, lanes], number], axis=1)
             score_grad[flat, lanes] = (nt(left, right) * probs[flat, lanes].astype(F32)).astype(BF16)
 
+    copy_in(0, step_index).wait()
+    copy_in(1, step_index).wait()
     window_loop(score_step)
+    copy_in(0, following).start()
+    copy_in(2, step_index).wait()
     low_head = lax.broadcasted_iota(jnp.int32, (QUERIES, 128), 1) < DH
 
     def query_step(rows, near, flat, kind):
@@ -508,6 +512,8 @@
             total[pair, rows, :] = joined_heads(both, low_head)
 
     window_loop(query_step)
+    copy_in(2, following).start()
+    copy_in(3, step_index).wait()
     spread_up(total, 0.5)
 
     def take(at, scale, masked):
@@ -527,9 +533,9 @@
         row_loop(LEN, 64, take_step)
 
     take(0, 0.125, False)
-    for at, left, right, factor, scale, masked in (
-        (D, score_grad, query, 0.5, 0.125, False),
-        (2 * D, probs, numer, 1.0, 1.0, True),
+    for at, left, right, factor, scale, masked, index in (
+        (D, score_grad, query, 0.5, 0.125, False, 3),
+        (2 * D, probs, numer, 1.0, 1.0, True, 1),
     ):
         total[...] = jnp.zeros_like(total)
 
@@ -539,6 +545,7 @@
                 total[pair, near, :] += tn(left[flat, lanes], by_head(right[rows, lanes], half))
 
         window_loop(near_step)
+        copy_in(index, following).start()
         spread_up(total, factor)
         take(at, scale, masked)
 
@@ -568,8 +575,10 @@
 
     row_loop(LEN, 64, back_step)
 
-    @pl.when(step_index == pl.num_programs(0) - 1)
+    @pl.when(step_index == last)
     def _():
+        for index in range(4):
+            copy_in(index, last).wait()
         small = jnp.sum(sums[...].reshape(2, 8, D), axis=1)
         small = jnp.concatenate([small, jnp.zeros((6, D), F32)], axis=0).astype(BF16)
         for side, block, device in block_places(place, plain, 1):
@@ -612,9 +621,7 @@
 
 def attend(lengths, place, plain, tokens, blocks):
     count = lengths.shape[0]
-    levels = shape_of(count * ROWS, D, BF16)
     one = per_sequence(LEN, D)
-    all_levels = per_sequence(ROWS, D)
     flat = WINDOWS * 2 * QUERIES
     return pl.pallas_call(
         functools.partial(attend_kernel, plain),
@@ -629,23 +636,26 @@
             whole(POOL_CHUNK, POOL_CHUNK),
             whole(2, 128),
         ],
-        out_specs=[all_levels] * 3
-        + [per_sequence(flat, D), one, one, whole(3 * D, D), whole(8, D)],
-        out_shape=[levels] * 3
+        out_specs=[pl.BlockSpec(memory_space=pl.ANY)] * 4
+        + [one, one, whole(3 * D, D), whole(8, D)],
+        out_shape=[jax.ShapeDtypeStruct((count, ROWS, D), BF16)] * 3
         + [
-            shape_of(count * flat, D, BF16),
+            jax.ShapeDtypeStruct((count, flat, D), BF16),
             shape_of(count * LEN, D, BF16),
             shape_of(count * LEN, D, F32),
             shape_of(3 * D, D, BF16),
             shape_of(8, D, F32),
         ],
-        scratch_shapes=[
+        scratch_shapes=[vmem(ROWS, D, BF16)] * 3
+        + [
+            vmem(flat, D, BF16),
             vmem(LEN, D, BF16),
             vmem(LEN, 3 * D, BF16),
             vmem(SIZES[-1], 3 * D, F32),
             vmem(ROWS, 128, BF16),
             pltpu.VMEM((4, ROWS, 128), F32),
             pltpu.VMEM((4, ROWS, 128), F32),
+            pltpu.SemaphoreType.DMA((4,)),
         ],
         compiler_params=PARAMS,
         cost_estimate=cost(40),
@@ -669,7 +679,7 @@
     return pl.pallas_call(
         functools.partial(feed_kernel, plain),
         grid=(rows // LEN,),
-        in_specs=[SMEM] + [one] * 4 + [whole(16, SECOND_ROWS, D)] * 2,
+        in_specs=[SMEM] + [one] * 4 + [whole(4, SECOND_ROWS, D)] * 8,
         out_specs=[one] * 4 + [grads] * 4,
         out_shape=[low] * 4 + [jax.ShapeDtypeStruct((8, SECOND_ROWS, D), BF16)] * 4,
         scratch_shapes=[
@@ -700,7 +710,6 @@
 def attend_back(lengths, place, plain, tokens, middle_grad, numer_grad, total_grad, kept):
     count = lengths.shape[0]
     one = per_sequence(LEN, D)
-    all_levels = per_sequence(ROWS, D)
     flat = WINDOWS * 2 * QUERIES
     grads = whole(16, FIRST_ROWS, D)
     return pl.pallas_call(
@@ -708,8 +717,7 @@
         grid=(count,),
         in_specs=[SMEM, SMEM]
         + [one] * 4
-        + [all_levels] * 3
-        + [per_sequence(flat, D)]
+        + [pl.BlockSpec(memory_space=pl.ANY)] * 4
         + [whole(3 * D, D), whole(8, D), whole(POOL_CHUNK, POOL_CHUNK), whole(2, 128)],
         out_specs=[one, grads, grads],
         out_shape=[shape_of(count * LEN, D, BF16)]
@@ -725,6 +733,11 @@
             vmem(SIZES[-1], D, F32),
             vmem(16, D, F32),
             vmem(3 * D, D, F32),
+            vmem(ROWS, D, BF16),
+            vmem(ROWS, D, BF16),
+            vmem(ROWS, D, BF16),
+            vmem(flat, D, BF16),
+            pltpu.SemaphoreType.DMA((4,)),
         ],
         compiler_params=PARAMS,
         cost_estimate=cost(60),
@@ -858,19 +871,17 @@
 def exchange_permutes(place, tokens, lengths, weights, vectors, cotangent):
     first, second = pack(place, weights, vectors)
     rows = gather_rows(first)
-    in_x, in_y = across(rows, 2), across(rows, 4)
-    diagonal = jnp.concatenate([across(in_x[:2], 4), across(in_y[2:], 2)])
-    near = jnp.concatenate([rows, in_x, in_y, diagonal])
+    near = jnp.concatenate([rows] + [across(rows, bits) for bits in (2, 4, 6)])
     second_rows = gather_rows(second)
     near, second_rows = lax.optimization_barrier((near, second_rows))
     first_blocks = (near, across(near, 1))
     first_blocks, second_rows = lax.optimization_barrier((first_blocks, second_rows))
-    others = [across(second_rows, bits) for bits in (2, 4, 6)]
+    others = [across(second_rows, bits) for bits in (2, 4, 6)] + [across(second_rows, 1)]
     *kept, attn, total, weights, gains = attend(lengths, place, False, tokens, first_blocks)
     kept += [weights, gains]
     attn, total, others = lax.optimization_barrier((attn, total, others))
-    near = jnp.concatenate([second_rows] + others)
-    second_blocks = (near, across(near, 1))
+    *others, partner = others
+    second_blocks = [second_rows, *others, partner] + [across(other, 1) for other in others]
     output, middle_grad, numer_grad, total_grad, *parts = feed(
         place, False, tokens, attn, total, cotangent, second_blocks
     )
@@ -878,10 +889,11 @@
     grad_tokens, near, far = attend_back(
         lengths, place, False, tokens, middle_grad, numer_grad, total_grad, kept
     )
-    near, far, others = lax.optimization_barrier((near, far, others))
+    partner = across(far, 1)
+    near, partner, others = lax.optimization_barrier((near, partner, others))
     second = added([parts[0]] + others).astype(BF16)
     second = added([second[:4], across(second[4:], 1)]).astype(BF16)
-    first = added([near, across(far, 1)]).astype(BF16).reshape(4, 4, FIRST_ROWS, D)
+    first = added([near, partner]).astype(BF16).reshape(4, 4, FIRST_ROWS, D)
     by_x, by_y = first[:, :2], first[:, 2:]
     sent_x = across(jnp.stack([by_x[1], by_x[3]]), 2)
     sent_y = across(jnp.stack([by_y[2], by_y[3]]), 4)
@@ -921,9 +933,9 @@
     up = lax.all_gather(w_up.T, AXES, axis=0, tiled=True).reshape(32, 4 * SHARE, D)
     down = lax.all_gather(w_down.T, AXES, axis=0, tiled=True).reshape(32, SHARE, 4, D)
     down = jnp.transpose(down, (0, 2, 1, 3)).reshape(32, 4 * SHARE, D)
-    second_blocks = halved(
-        [gathered(w_out.T), up, down, vector_rows([gain_ffn, shift_ffn, bias_down, bias_up])]
-    )
+    vectors = vector_rows([gain_ffn, shift_ffn, bias_down, bias_up])
+    second_blocks = jnp.concatenate([gathered(w_out.T), up, down, vectors], axis=1)
+    second_blocks = [second_blocks[at : at + 4] for at in range(0, 32, 4)]
     *kept, attn, total, weights, gains = attend(lengths, place, True, tokens, first_blocks)
     kept += [weights, gains]
     output, middle_grad, numer_grad, total_grad, *parts = feed(

time: 242 us -> 235 us (0.971)
  local copies, waits for them, and re-layouts: 7.81 us -> 3.06 us
  Pallas kernels: 153 us -> 149 us
    ppermute x12, waiting for transfers between devices: 14.2 us -> 20.5 us  [along(): return lax.ppermute(values, 'dp', [(i, (i + step) % 4) for i in range(4)])]
    ppermute x18 -> x20, waiting for transfers between devices: 22.7 us -> 16.5 us  [across(): return lax.ppermute(values, 'fsdp', [(i, i ^ bits) for i in range(8)])]
    ppermute x12, starting transfers between devices: 17.4 us -> 21.6 us  [along(): return lax.ppermute(values, 'dp', [(i, (i + step) % 4) for i in range(4)])]
    unnamed x32 -> x28, local copies, waits for them, and re-layouts: 5.21 us -> 1.61 us
    ppermute x18 -> x20, starting transfers between devices: 18.8 us -> 16 us  [across(): return lax.ppermute(values, 'fsdp', [(i, i ^ bits) for i in range(8)])]
  transfers between devices with their start and end apart: 30 -> 32, of which waited for: 13 -> 13; matrix products, arithmetic and copies ran while one was open for 2% -> 3% of each run, Pallas kernels for 35% -> 34%
where the time goes in v1:
time: 235 us
  Pallas kernels  149 us (63%)
  starting transfers between devices  37.6 us (16%)
  waiting for transfers between devices  37 us (16%)
  other arithmetic  7.07 us (3%)
  local copies, waits for them, and re-layouts  3.06 us (1%)
    pallas_call x1, Pallas kernels, feed(): pl.pallas_call(functools.partial(feed_kernel, plain), grid=(rows // LEN,)...  65.3 us
    pallas_call x1, Pallas kernels, attend_back(): pl.pallas_call(functools.partial(attend_back_kernel, plain), grid=(count,...  47.9 us
    pallas_call x1, Pallas kernels, attend(): pl.pallas_call(functools.partial(attend_kernel, plain), grid=(count,), in...  32.1 us
    ppermute x12, starting transfers between devices, along(): return lax.ppermute(values, 'dp', [(i, (i + step) % 4) for i in range(4)])  21.6 us
    ppermute x12, waiting for transfers between devices, along(): return lax.ppermute(values, 'dp', [(i, (i + step) % 4) for i in range(4)])  20.5 us
    ppermute x20, waiting for transfers between devices, across(): return lax.ppermute(values, 'fsdp', [(i, i ^ bits) for i in range(8)])  16.5 us
    ppermute x20, starting transfers between devices, across(): return lax.ppermute(values, 'fsdp', [(i, i ^ bits) for i in range(8)])  16 us
  transfers between devices with their start and end apart: 32, of which 13 were waited for; matrix products, arithmetic and copies ran while one was open for 3% of the time, Pallas kernels for 34%

profile of v1, /device:TPU:0, one launch (start us, length us, event | category | flops | bytes accessed | tf_op | source)
XLA Modules:
  0.0 235.1 jit_solution(828322681662898536)
XLA Ops:
  0.6 0.6 pad_add_fusion.place
  1.3 1.8 pack.1
  3.1 5.0 %collective-permute-start.2 = (bf16[56,512]{1,0:T(8,128)(2,1)}, bf16[56,512]{1,0:T(8,128)(2,1)S(1)}, u32[]{:S(2)}, u32[]{:S(2)}) collective-permute-start(bf16[56,512]{1,0:T(8,128)(2,1)} %get-tuple-element.63), channel_id=1, source_target_pairs={{0,24},{8,0},{16,8},{24,16},{1,25},{9,1},{17,9},{25,17},{2,26},{10... | collective-permute-start | bytes 172040 | tf_op jit(solution)/shard_map/ppermute | solution.py:805
  8.1 0.0 collective-permute-start.1
  8.1 1.0 collective-permute-start
  9.1 2.8 %collective-permute-start.8 = (bf16[152,512]{1,0:T(8,128)(2,1)}, bf16[152,512]{1,0:T(8,128)(2,1)S(1)}, u32[]{:S(2)}, u32[]{:S(2)}) collective-permute-start(bf16[152,512]{1,0:T(8,128)(2,1)} %get-tuple-element.64), channel_id=1, source_target_pairs={{0,24},{8,0},{16,8},{24,16},{1,25},{9,1},{17,9},{25,17},{2,26},{10... | collective-permute-start | bytes 466952 | tf_op jit(solution)/shard_map/ppermute | solution.py:805
  12.0 1.1 collective-permute-start.7
  13.1 0.8 constant_dynamic-update-slice_fusion.6
  13.9 0.0 collective-permute-start.6
  13.9 0.6 collective-permute-done.1
  14.5 0.5 collective-permute-done
  15.0 0.8 pad_maximum_fusion.1
  15.8 2.5 %collective-permute-start.5 = (bf16[4,56,512]{2,1,0:T(8,128)(2,1)S(1)}, bf16[4,56,512]{2,1,0:T(8,128)(2,1)S(1)}, u32[]{:S(2)}, u32[]{:S(2)}) collective-permute-start(bf16[4,56,512]{2,1,0:T(8,128)(2,1)S(1)} %pad_maximum_fusion.1), channel_id=1, source_target_pairs={{0,6},{1,7},{2,4},{3,5},{4,2},{5,3},{6,0},{7,1},{8,14},{9,15},{10,... | collective-permute-start | bytes 688136 | tf_op jit(solution)/shard_map/ppermute | solution.py:801
  18.3 0.5 collective-permute-start.3
  18.9 0.6 collective-permute-start.4
  19.5 8.0 %collective-permute-done.7 = bf16[152,512]{1,0:T(8,128)(2,1)S(1)} collective-permute-done((bf16[152,512]{1,0:T(8,128)(2,1)}, bf16[152,512]{1,0:T(8,128)(2,1)S(1)}, u32[]{:S(2)}, u32[]{:S(2)}) %collective-permute-start.7) | collective-permute-done | bytes 155680 | tf_op jit(solution)/shard_map/ppermute | solution.py:805
  27.5 1.0 pad_maximum_fusion.refs_0_
  28.6 0.0 copy-start.2
  28.6 0.1 collective-permute-start.9
  28.7 2.5 %collective-permute-done.9.far_blocks = bf16[16,56,512]{2,1,0:T(8,128)(2,1)S(1)} collective-permute-done((bf16[16,56,512]{2,1,0:T(8,128)(2,1)S(1)}, bf16[16,56,512]{2,1,0:T(8,128)(2,1)S(1)}, u32[]{:S(2)}, u32[]{:S(2)}) %collective-permute-start.9) | collective-permute-done | bytes 917536 | tf_op jit(solution)/shard_map/ppermute | solution.py:801
  31.2 0.1 collective-permute-start.13
  31.3 2.5 %collective-permute-start.12 = (bf16[4,152,512]{2,1,0:T(8,128)(2,1)S(1)}, bf16[4,152,512]{2,1,0:T(8,128)(2,1)}, u32[]{:S(2)}, u32[]{:S(2)}) collective-permute-start(bf16[4,152,512]{2,1,0:T(8,128)(2,1)S(1)} %pad_maximum_fusion.refs_0_), channel_id=1, source_target_pairs={{0,6},{1,7},{2,4},{3,5},{4,2},{5,3},{6,0},{7,1},{8,14},{9,15},{10,... | collective-permute-start | bytes 1867784 | tf_op jit(solution)/shard_map/ppermute | solution.py:801
  33.8 0.5 collective-permute-start.11
  34.3 0.5 collective-permute-start.10
  34.8 32.1 %attend.1 = (bf16[3,2192,512]{2,1,0:T(8,128)(2,1)}, bf16[3,2192,512]{2,1,0:T(8,128)(2,1)}, bf16[3,2192,512]{2,1,0:T(8,128)(2,1)}, bf16[3,4096,512]{2,1,0:T(8,128...) custom-call(s32[3]{0:T(128)} %lengths.3, ...), custom_call_target="tpu_custom_call" | custom-call | flops 40000000000 | bytes 40000000 | tf_op jit(solution)/shard_map/attend/pallas_call | solution.py:626
  67.0 0.1 collective-permute-start.14
  67.1 0.5 collective-permute-start.15
  67.6 0.1 collective-permute-start.16
  67.7 1.8 collective-permute-done.14.refs_5_
  69.4 0.9 collective-permute-done.15.refs_6_
  70.3 0.9 collective-permute-done.16.refs_7_
  71.2 65.3 %feed.1 = (bf16[3072,512]{1,0:T(8,128)(2,1)}, bf16[3072,512]{1,0:T(8,128)(2,1)}, bf16[3072,512]{1,0:T(8,128)(2,1)}, bf16[3072,512]{1,0:T(8,128)(2,1)}, bf16[8,15...) custom-call(s32[2]{0:T(128)} %pad_add_fusion.place, ...), custom_call_target="tpu_custom_call" | custom-call | flops 74999996416 | bytes 75000000 | tf_op jit(solution)/shard_map/feed/pallas_call | solution.py:679
  136.5 1.6 collective-permute-start.18
  138.1 1.5 collective-permute-start.19
  139.6 0.5 collective-permute-start.20
  140.1 47.9 %attend_back.1 = (bf16[3072,512]{1,0:T(8,128)(2,1)}, bf16[16,56,512]{2,1,0:T(8,128)(2,1)}, bf16[16,56,512]{2,1,0:T(8,128)(2,1)}) custom-call(s32[3]{0:T(128)} %lengths.3, s32[2]{0:T(128)} %pad_add_fusion.place, bf16[3072,512]{1,0:T(8,128)(2,1)} %tokens.5, bf16[3072,512]{1,0:T(8,128)(2,1)} %get-tuple-element.79.middle_grad, ...), custom_call_target="tpu_custom_call" | custom-call | flops 60000002048 | bytes 60000000 | tf_op jit(solution)/shard_map/attend_back/pallas_call | solution.py:715
  188.0 0.1 collective-permute-start.17
  188.0 2.7 %collective-permute-done.17 = bf16[16,56,512]{2,1,0:T(8,128)(2,1)S(1)} collective-permute-done((bf16[16,56,512]{2,1,0:T(8,128)(2,1)}, bf16[16,56,512]{2,1,0:T(8,128)(2,1)S(1)}, u32[]{:S(2)}, u32[]{:S(2)}) %collective-permute-start.17) | collective-permute-done | bytes 917536 | tf_op jit(solution)/shard_map/ppermute | solution.py:801
  190.7 3.5 %collective-permute-done.19 = bf16[8,152,512]{2,1,0:T(8,128)(2,1)} collective-permute-done((bf16[8,152,512]{2,1,0:T(8,128)(2,1)}, bf16[8,152,512]{2,1,0:T(8,128)(2,1)}, u32[]{:S(2)}, u32[]{:S(2)}) %collective-permute-start.19) | collective-permute-done | bytes 1245216 | tf_op jit(solution)/shard_map/ppermute | solution.py:801
  194.2 1.5 add_convert_fusion.1
  195.8 1.6 collective-permute-start.24
  197.4 0.6 collective-permute-start.21
  198.0 2.7 %add_convert_fusion = bf16[8,152,512]{2,1,0:T(8,128)(2,1)S(1)} fusion(bf16[8,152,512]{2,1,0:T(8,128)(2,1)} %collective-permute-done.20, bf16[8,152,512]{2,1,0:T(8,128)(2,1)} %collective-permute-done.19, bf16[8,152,512]{2,1,0:T(8,128)(2,1)} %collective-permute-done.18, bf16[8,152,512]{2,1,0:T(8,128)(2,1)S(1)} %copy-done), kind=kLoop, calls=%fused_computation | loop fusion | flops 4980736 | bytes 6225920 | tf_op jit(solution)/shard_map/convert_element_type | solution.py:894
  200.8 0.1 collective-permute-start.28
  200.9 1.6 collective-permute-done.24
  202.5 0.1 add_convert_fusion.3
  202.6 1.5 collective-permute-start.25
  204.1 0.1 add_convert_fusion.4
  204.2 0.6 collective-permute-start.22
  204.8 2.6 %collective-permute-done.25 = bf16[2,56,512]{2,1,0:T(8,128)(2,1)S(1)} collective-permute-done((bf16[2,56,512]{2,1,0:T(8,128)(2,1)S(1)}, bf16[2,56,512]{2,1,0:T(8,128)(2,1)S(1)}, u32[]{:S(2)}, u32[]{:S(2)}) %collective-permute-start.25) | collective-permute-done | bytes 114720 | tf_op jit(solution)/shard_map/ppermute | solution.py:801
  207.5 1.6 collective-permute-start.27
  209.1 5.1 %collective-permute-start.26 = (bf16[56,512]{1,0:T(8,128)(2,1)S(1)}, bf16[56,512]{1,0:T(8,128)(2,1)S(1)}, u32[]{:S(2)}, u32[]{:S(2)}) collective-permute-start(bf16[56,512]{1,0:T(8,128)(2,1)S(1)} %get-tuple-element.121), channel_id=1, source_target_pairs={{0,16},{8,24},{16,0},{24,8},{1,17},{9,25},{17,1},{25,9},{2,18},{10... | collective-permute-start | bytes 172040 | tf_op jit(solution)/shard_map/ppermute | solution.py:805
  214.3 0.2 add_convert_fusion.2
  214.5 0.7 slice_bitcast_fusion
  215.2 1.4 collective-permute-start.31
  216.5 2.0 collective-permute-start.30
  218.6 0.0 collective-permute-start.29
  218.6 0.6 slice_bitcast_fusion.10
  219.2 1.4 collective-permute-start.23
  220.7 8.2 %collective-permute-done.23.refs_1_ = bf16[56,512]{1,0:T(8,128)(2,1)S(1)} collective-permute-done((bf16[56,512]{1,0:T(8,128)(2,1)S(1)}, bf16[56,512]{1,0:T(8,128)(2,1)S(1)}, u32[]{:S(2)}, u32[]{:S(2)}) %collective-permute-start.23) | collective-permute-done | bytes 57376 | tf_op jit(solution)/shard_map/ppermute | solution.py:805
  228.9 3.3 %collective-permute-done.30.refs_6_ = bf16[152,512]{1,0:T(8,128)(2,1)S(1)} collective-permute-done((bf16[152,512]{1,0:T(8,128)(2,1)S(1)}, bf16[152,512]{1,0:T(8,128)(2,1)S(1)}, u32[]{:S(2)}, u32[]{:S(2)}) %collective-permute-start.30) | collective-permute-done | bytes 155680 | tf_op jit(solution)/shard_map/ppermute | solution.py:805
  232.2 0.6 copy-done.6
  232.8 0.1 copy-done.7
  232.9 2.0 finish.1
  (53 shorter events, 0.4 us)
Async XLA Ops:
  3.1 10.8 %collective-permute-start.2 = (bf16[56,512]{1,0:T(8,128)(2,1)}, bf16[56,512]{1,0:T(8,128)(2,1)S(1)}, u32[]{:S(2)}, u32[]{:S(2)}) collective-permute-start(bf16[56,512]{1,0:T(8,128)(2,1)} %get-tuple-element.63), channel_id=1, source_target_pairs={{0,24},{8,0},{16,8},{24,16},{1,25},{9,1},{17,9},{25,17},{2,26},{10... | collective-permute-start | bytes 172040 | tf_op jit(solution)/shard_map/ppermute | solution.py:805
  8.1 6.4 %collective-permute-start.1 = (bf16[56,512]{1,0:T(8,128)(2,1)}, bf16[56,512]{1,0:T(8,128)(2,1)S(1)}, u32[]{:S(2)}, u32[]{:S(2)}) collective-permute-start(bf16[56,512]{1,0:T(8,128)(2,1)} %get-tuple-element.63), channel_id=1, source_target_pairs={{0,16},{8,24},{16,0},{24,8},{1,17},{9,25},{17,1},{25,9},{2,18},{10... | collective-permute-start | bytes 172040 | tf_op jit(solution)/shard_map/ppermute | solution.py:805
  8.1 6.9 %collective-permute-start = (bf16[56,512]{1,0:T(8,128)(2,1)}, bf16[56,512]{1,0:T(8,128)(2,1)S(1)}, u32[]{:S(2)}, u32[]{:S(2)}) collective-permute-start(bf16[56,512]{1,0:T(8,128)(2,1)} %get-tuple-element.63), channel_id=1, source_target_pairs={{0,8},{8,16},{16,24},{24,0},{1,9},{9,17},{17,25},{25,1},{2,10},{10... | collective-permute-start | bytes 172040 | tf_op jit(solution)/shard_map/ppermute | solution.py:805
  9.1 9.8 %collective-permute-start.8 = (bf16[152,512]{1,0:T(8,128)(2,1)}, bf16[152,512]{1,0:T(8,128)(2,1)S(1)}, u32[]{:S(2)}, u32[]{:S(2)}) collective-permute-start(bf16[152,512]{1,0:T(8,128)(2,1)} %get-tuple-element.64), channel_id=1, source_target_pairs={{0,24},{8,0},{16,8},{24,16},{1,25},{9,1},{17,9},{25,17},{2,26},{10... | collective-permute-start | bytes 466952 | tf_op jit(solution)/shard_map/ppermute | solution.py:805
  12.0 15.5 %collective-permute-start.7 = (bf16[152,512]{1,0:T(8,128)(2,1)}, bf16[152,512]{1,0:T(8,128)(2,1)S(1)}, u32[]{:S(2)}, u32[]{:S(2)}) collective-permute-start(bf16[152,512]{1,0:T(8,128)(2,1)} %get-tuple-element.64), channel_id=1, source_target_pairs={{0,16},{8,24},{16,0},{24,8},{1,17},{9,25},{17,1},{25,9},{2,18},{10... | collective-permute-start | bytes 466952 | tf_op jit(solution)/shard_map/ppermute | solution.py:805
  13.9 13.6 %collective-permute-start.6 = (bf16[152,512]{1,0:T(8,128)(2,1)}, bf16[152,512]{1,0:T(8,128)(2,1)S(1)}, u32[]{:S(2)}, u32[]{:S(2)}) collective-permute-start(bf16[152,512]{1,0:T(8,128)(2,1)} %get-tuple-element.64), channel_id=1, source_target_pairs={{0,8},{8,16},{16,24},{24,0},{1,9},{9,17},{17,25},{25,1},{2,10},{10... | collective-permute-start | bytes 466952 | tf_op jit(solution)/shard_map/ppermute | solution.py:805
  15.8 12.7 %collective-permute-start.5 = (bf16[4,56,512]{2,1,0:T(8,128)(2,1)S(1)}, bf16[4,56,512]{2,1,0:T(8,128)(2,1)S(1)}, u32[]{:S(2)}, u32[]{:S(2)}) collective-permute-start(bf16[4,56,512]{2,1,0:T(8,128)(2,1)S(1)} %pad_maximum_fusion.1), channel_id=1, source_target_pairs={{0,6},{1,7},{2,4},{3,5},{4,2},{5,3},{6,0},{7,1},{8,14},{9,15},{10,... | collective-permute-start | bytes 688136 | tf_op jit(solution)/shard_map/ppermute | solution.py:801
  18.3 10.2 %collective-permute-start.3 = (bf16[4,56,512]{2,1,0:T(8,128)(2,1)S(1)}, bf16[4,56,512]{2,1,0:T(8,128)(2,1)S(1)}, u32[]{:S(2)}, u32[]{:S(2)}) collective-permute-start(bf16[4,56,512]{2,1,0:T(8,128)(2,1)S(1)} %pad_maximum_fusion.1), channel_id=1, source_target_pairs={{0,2},{1,3},{2,0},{3,1},{4,6},{5,7},{6,4},{7,5},{8,10},{9,11},{10,... | collective-permute-start | bytes 688136 | tf_op jit(solution)/shard_map/ppermute | solution.py:801
  18.9 9.6 %collective-permute-start.4 = (bf16[4,56,512]{2,1,0:T(8,128)(2,1)S(1)}, bf16[4,56,512]{2,1,0:T(8,128)(2,1)S(1)}, u32[]{:S(2)}, u32[]{:S(2)}) collective-permute-start(bf16[4,56,512]{2,1,0:T(8,128)(2,1)S(1)} %pad_maximum_fusion.1), channel_id=1, source_target_pairs={{0,4},{1,5},{2,6},{3,7},{4,0},{5,1},{6,2},{7,3},{8,12},{9,13},{10,... | collective-permute-start | bytes 688136 | tf_op jit(solution)/shard_map/ppermute | solution.py:801
  28.5 38.5 %copy-start.1 = (bf16[4,152,512]{2,1,0:T(8,128)(2,1)}, bf16[4,152,512]{2,1,0:T(8,128)(2,1)S(1)}, u32[]{:S(2)}) copy-start(bf16[4,152,512]{2,1,0:T(8,128)(2,1)S(1)} %pad_maximum_fusion.refs_0_) | copy-start | bytes 1867780
  28.6 5.2 %copy-start.2 = (bf16[16,56,512]{2,1,0:T(8,128)(2,1)}, bf16[16,56,512]{2,1,0:T(8,128)(2,1)S(1)}, u32[]{:S(2)}) copy-start(bf16[16,56,512]{2,1,0:T(8,128)(2,1)S(1)} %constant_dynamic-update-slice_fusion.near_blocks) | copy-start | bytes 2752516
  28.6 2.5 %collective-permute-start.9 = (bf16[16,56,512]{2,1,0:T(8,128)(2,1)S(1)}, bf16[16,56,512]{2,1,0:T(8,128)(2,1)S(1)}, u32[]{:S(2)}, u32[]{:S(2)}) collective-permute-start(bf16[16,56,512]{2,1,0:T(8,128)(2,1)S(1)} %constant_dynamic-update-slice_fusion.near_blocks), channel_id=1, source_target_pairs={{0,1},{1,0},{2,3},{3,2},{4,5},{5,4},{6,7},{7,6},{8,9},{9,8},{10,11... | collective-permute-start | bytes 2752520 | tf_op jit(solution)/shard_map/ppermute | solution.py:801
  31.2 3.1 %copy-start.3 = (bf16[16,56,512]{2,1,0:T(8,128)(2,1)}, bf16[16,56,512]{2,1,0:T(8,128)(2,1)S(1)}, u32[]{:S(2)}) copy-start(bf16[16,56,512]{2,1,0:T(8,128)(2,1)S(1)} %collective-permute-done.9.far_blocks) | copy-start | bytes 2752516
  31.2 35.8 %collective-permute-start.13 = (bf16[4,152,512]{2,1,0:T(8,128)(2,1)S(1)}, bf16[4,152,512]{2,1,0:T(8,128)(2,1)}, u32[]{:S(2)}, u32[]{:S(2)}) collective-permute-start(bf16[4,152,512]{2,1,0:T(8,128)(2,1)S(1)} %pad_maximum_fusion.refs_0_), channel_id=1, source_target_pairs={{0,1},{1,0},{2,3},{3,2},{4,5},{5,4},{6,7},{7,6},{8,9},{9,8},{10,11... | collective-permute-start | bytes 1867784 | tf_op jit(solution)/shard_map/ppermute | solution.py:801
  31.3 35.7 %collective-permute-start.12 = (bf16[4,152,512]{2,1,0:T(8,128)(2,1)S(1)}, bf16[4,152,512]{2,1,0:T(8,128)(2,1)}, u32[]{:S(2)}, u32[]{:S(2)}) collective-permute-start(bf16[4,152,512]{2,1,0:T(8,128)(2,1)S(1)} %pad_maximum_fusion.refs_0_), channel_id=1, source_target_pairs={{0,6},{1,7},{2,4},{3,5},{4,2},{5,3},{6,0},{7,1},{8,14},{9,15},{10,... | collective-permute-start | bytes 1867784 | tf_op jit(solution)/shard_map/ppermute | solution.py:801
  33.8 33.2 %collective-permute-start.11 = (bf16[4,152,512]{2,1,0:T(8,128)(2,1)S(1)}, bf16[4,152,512]{2,1,0:T(8,128)(2,1)}, u32[]{:S(2)}, u32[]{:S(2)}) collective-permute-start(bf16[4,152,512]{2,1,0:T(8,128)(2,1)S(1)} %pad_maximum_fusion.refs_0_), channel_id=1, source_target_pairs={{0,4},{1,5},{2,6},{3,7},{4,0},{5,1},{6,2},{7,3},{8,12},{9,13},{10,... | collective-permute-start | bytes 1867784 | tf_op jit(solution)/shard_map/ppermute | solution.py:801
  34.3 32.7 %collective-permute-start.10 = (bf16[4,152,512]{2,1,0:T(8,128)(2,1)S(1)}, bf16[4,152,512]{2,1,0:T(8,128)(2,1)}, u32[]{:S(2)}, u32[]{:S(2)}) collective-permute-start(bf16[4,152,512]{2,1,0:T(8,128)(2,1)S(1)} %pad_maximum_fusion.refs_0_), channel_id=1, source_target_pairs={{0,2},{1,3},{2,0},{3,1},{4,6},{5,7},{6,4},{7,5},{8,10},{9,11},{10,... | collective-permute-start | bytes 1867784 | tf_op jit(solution)/shard_map/ppermute | solution.py:801
  67.0 2.4 %collective-permute-start.14 = (bf16[4,152,512]{2,1,0:T(8,128)(2,1)}, bf16[4,152,512]{2,1,0:T(8,128)(2,1)S(1)}, u32[]{:S(2)}, u32[]{:S(2)}) collective-permute-start(bf16[4,152,512]{2,1,0:T(8,128)(2,1)} %collective-permute-done.10.refs_1_), channel_id=1, source_target_pairs={{0,1},{1,0},{2,3},{3,2},{4,5},{5,4},{6,7},{7,6},{8,9},{9,8},{10,11... | collective-permute-start | bytes 1867784 | tf_op jit(solution)/shard_map/ppermute | solution.py:801
  67.1 3.3 %collective-permute-start.15 = (bf16[4,152,512]{2,1,0:T(8,128)(2,1)}, bf16[4,152,512]{2,1,0:T(8,128)(2,1)}, u32[]{:S(2)}, u32[]{:S(2)}) collective-permute-start(bf16[4,152,512]{2,1,0:T(8,128)(2,1)} %collective-permute-done.11.refs_2_), channel_id=1, source_target_pairs={{0,1},{1,0},{2,3},{3,2},{4,5},{5,4},{6,7},{7,6},{8,9},{9,8},{10,11... | collective-permute-start | bytes 1867784 | tf_op jit(solution)/shard_map/ppermute | solution.py:801
  67.6 3.7 %collective-permute-start.16 = (bf16[4,152,512]{2,1,0:T(8,128)(2,1)}, bf16[4,152,512]{2,1,0:T(8,128)(2,1)}, u32[]{:S(2)}, u32[]{:S(2)}) collective-permute-start(bf16[4,152,512]{2,1,0:T(8,128)(2,1)} %collective-permute-done.12.refs_3_), channel_id=1, source_target_pairs={{0,1},{1,0},{2,3},{3,2},{4,5},{5,4},{6,7},{7,6},{8,9},{9,8},{10,11... | collective-permute-start | bytes 1867784 | tf_op jit(solution)/shard_map/ppermute | solution.py:801
  69.4 1.8 copy-start.4
  136.5 54.2 %collective-permute-start.18 = (bf16[8,152,512]{2,1,0:T(8,128)(2,1)}, bf16[8,152,512]{2,1,0:T(8,128)(2,1)}, u32[]{:S(2)}, u32[]{:S(2)}) collective-permute-start(bf16[8,152,512]{2,1,0:T(8,128)(2,1)} %get-tuple-element.91), channel_id=1, source_target_pairs={{0,2},{1,3},{2,0},{3,1},{4,6},{5,7},{6,4},{7,5},{8,10},{9,11},{10,... | collective-permute-start | bytes 3735560 | tf_op jit(solution)/shard_map/ppermute | solution.py:801
  138.1 56.1 %collective-permute-start.19 = (bf16[8,152,512]{2,1,0:T(8,128)(2,1)}, bf16[8,152,512]{2,1,0:T(8,128)(2,1)}, u32[]{:S(2)}, u32[]{:S(2)}) collective-permute-start(bf16[8,152,512]{2,1,0:T(8,128)(2,1)} %get-tuple-element.92), channel_id=1, source_target_pairs={{0,4},{1,5},{2,6},{3,7},{4,0},{5,1},{6,2},{7,3},{8,12},{9,13},{10,... | collective-permute-start | bytes 3735560 | tf_op jit(solution)/shard_map/ppermute | solution.py:801
  139.6 54.6 %collective-permute-start.20 = (bf16[8,152,512]{2,1,0:T(8,128)(2,1)}, bf16[8,152,512]{2,1,0:T(8,128)(2,1)}, u32[]{:S(2)}, u32[]{:S(2)}) collective-permute-start(bf16[8,152,512]{2,1,0:T(8,128)(2,1)} %get-tuple-element.93), channel_id=1, source_target_pairs={{0,6},{1,7},{2,4},{3,5},{4,2},{5,3},{6,0},{7,1},{8,14},{9,15},{10,... | collective-permute-start | bytes 3735560 | tf_op jit(solution)/shard_map/ppermute | solution.py:801
  188.0 2.7 %collective-permute-start.17 = (bf16[16,56,512]{2,1,0:T(8,128)(2,1)}, bf16[16,56,512]{2,1,0:T(8,128)(2,1)S(1)}, u32[]{:S(2)}, u32[]{:S(2)}) collective-permute-start(bf16[16,56,512]{2,1,0:T(8,128)(2,1)} %get-tuple-element.90), channel_id=1, source_target_pairs={{0,1},{1,0},{2,3},{3,2},{4,5},{5,4},{6,7},{7,6},{8,9},{9,8},{10,11... | collective-permute-start | bytes 2752520 | tf_op jit(solution)/shard_map/ppermute | solution.py:801
  194.2 3.8 %copy-start = (bf16[8,152,512]{2,1,0:T(8,128)(2,1)S(1)}, bf16[8,152,512]{2,1,0:T(8,128)(2,1)}, u32[]{:S(2)}) copy-start(bf16[8,152,512]{2,1,0:T(8,128)(2,1)} %get-tuple-element.96) | copy-start | bytes 3735556
  195.8 6.7 %collective-permute-start.24 = (bf16[2,2,56,512]{3,2,1,0:T(8,128)(2,1)S(1)}, bf16[2,2,56,512]{3,2,1,0:T(8,128)(2,1)S(1)}, u32[]{:S(2)}, u32[]{:S(2)}) collective-permute-start(bf16[2,2,56,512]{3,2,1,0:T(8,128)(2,1)S(1)} %stack.69), channel_id=1, source_target_pairs={{0,4},{1,5},{2,6},{3,7},{4,0},{5,1},{6,2},{7,3},{8,12},{9,13},{10,... | collective-permute-start | bytes 688136 | tf_op jit(solution)/shard_map/ppermute | solution.py:801
  197.4 6.6 %collective-permute-start.21 = (bf16[2,2,56,512]{3,2,1,0:T(8,128)(2,1)S(1)}, bf16[2,2,56,512]{3,2,1,0:T(8,128)(2,1)S(1)}, u32[]{:S(2)}, u32[]{:S(2)}) collective-permute-start(bf16[2,2,56,512]{3,2,1,0:T(8,128)(2,1)S(1)} %pad_maximum_fusion.2), channel_id=1, source_target_pairs={{0,2},{1,3},{2,0},{3,1},{4,6},{5,7},{6,4},{7,5},{8,10},{9,11},{10,... | collective-permute-start | bytes 688136 | tf_op jit(solution)/shard_map/ppermute | solution.py:801
  200.8 13.5 %collective-permute-start.28 = (bf16[4,152,512]{2,1,0:T(8,128)(2,1)S(1)}, bf16[4,152,512]{2,1,0:T(8,128)(2,1)S(1)}, u32[]{:S(2)}, u32[]{:S(2)}) collective-permute-start(bf16[4,152,512]{2,1,0:T(8,128)(2,1)S(1)} %slice.101), channel_id=1, source_target_pairs={{0,1},{1,0},{2,3},{3,2},{4,5},{5,4},{6,7},{7,6},{8,9},{9,8},{10,11... | collective-permute-start | bytes 1867784 | tf_op jit(solution)/shard_map/ppermute | solution.py:801
  202.6 4.9 %collective-permute-start.25 = (bf16[2,56,512]{2,1,0:T(8,128)(2,1)S(1)}, bf16[2,56,512]{2,1,0:T(8,128)(2,1)S(1)}, u32[]{:S(2)}, u32[]{:S(2)}) collective-permute-start(bf16[2,56,512]{2,1,0:T(8,128)(2,1)S(1)} %slice_bitcast_fusion.4), channel_id=1, source_target_pairs={{0,2},{1,3},{2,0},{3,1},{4,6},{5,7},{6,4},{7,5},{8,10},{9,11},{10,... | collective-permute-start | bytes 344072 | tf_op jit(solution)/shard_map/ppermute | solution.py:801
  204.2 10.1 %collective-permute-start.22 = (bf16[2,56,512]{2,1,0:T(8,128)(2,1)S(1)}, bf16[2,56,512]{2,1,0:T(8,128)(2,1)S(1)}, u32[]{:S(2)}, u32[]{:S(2)}) collective-permute-start(bf16[2,56,512]{2,1,0:T(8,128)(2,1)S(1)} %slice_bitcast_fusion.6), channel_id=1, source_target_pairs={{0,4},{1,5},{2,6},{3,7},{4,0},{5,1},{6,2},{7,3},{8,12},{9,13},{10,... | collective-permute-start | bytes 344072 | tf_op jit(solution)/shard_map/ppermute | solution.py:801
  207.5 11.7 %collective-permute-start.27 = (bf16[56,512]{1,0:T(8,128)(2,1)S(1)}, bf16[56,512]{1,0:T(8,128)(2,1)S(1)}, u32[]{:S(2)}, u32[]{:S(2)}) collective-permute-start(bf16[56,512]{1,0:T(8,128)(2,1)S(1)} %get-tuple-element.120), channel_id=1, source_target_pairs={{0,24},{8,0},{16,8},{24,16},{1,25},{9,1},{17,9},{25,17},{2,26},{10... | collective-permute-start | bytes 172040 | tf_op jit(solution)/shard_map/ppermute | solution.py:805
  209.1 11.6 %collective-permute-start.26 = (bf16[56,512]{1,0:T(8,128)(2,1)S(1)}, bf16[56,512]{1,0:T(8,128)(2,1)S(1)}, u32[]{:S(2)}, u32[]{:S(2)}) collective-permute-start(bf16[56,512]{1,0:T(8,128)(2,1)S(1)} %get-tuple-element.121), channel_id=1, source_target_pairs={{0,16},{8,24},{16,0},{24,8},{1,17},{9,25},{17,1},{25,9},{2,18},{10... | collective-permute-start | bytes 172040 | tf_op jit(solution)/shard_map/ppermute | solution.py:805
  215.2 13.7 %collective-permute-start.31 = (bf16[152,512]{1,0:T(8,128)(2,1)S(1)}, bf16[152,512]{1,0:T(8,128)(2,1)S(1)}, u32[]{:S(2)}, u32[]{:S(2)}) collective-permute-start(bf16[152,512]{1,0:T(8,128)(2,1)S(1)} %get-tuple-element.116), channel_id=1, source_target_pairs={{0,24},{8,0},{16,8},{24,16},{1,25},{9,1},{17,9},{25,17},{2,26},{10... | collective-permute-start | bytes 466952 | tf_op jit(solution)/shard_map/ppermute | solution.py:805
  216.5 15.6 %collective-permute-start.30 = (bf16[152,512]{1,0:T(8,128)(2,1)S(1)}, bf16[152,512]{1,0:T(8,128)(2,1)S(1)}, u32[]{:S(2)}, u32[]{:S(2)}) collective-permute-start(bf16[152,512]{1,0:T(8,128)(2,1)S(1)} %get-tuple-element.117), channel_id=1, source_target_pairs={{0,16},{8,24},{16,0},{24,8},{1,17},{9,25},{17,1},{25,9},{2,18},{10... | collective-permute-start | bytes 466952 | tf_op jit(solution)/shard_map/ppermute | solution.py:805
  218.6 13.6 %collective-permute-start.29 = (bf16[152,512]{1,0:T(8,128)(2,1)S(1)}, bf16[152,512]{1,0:T(8,128)(2,1)S(1)}, u32[]{:S(2)}, u32[]{:S(2)}) collective-permute-start(bf16[152,512]{1,0:T(8,128)(2,1)S(1)} %get-tuple-element.118), channel_id=1, source_target_pairs={{0,8},{8,16},{16,24},{24,0},{1,9},{9,17},{17,25},{25,1},{2,10},{10... | collective-permute-start | bytes 466952 | tf_op jit(solution)/shard_map/ppermute | solution.py:805
  219.2 12.9 %copy-start.8 = (bf16[56,512]{1,0:T(8,128)(2,1)}, bf16[56,512]{1,0:T(8,128)(2,1)S(1)}, u32[]{:S(2)}) copy-start(bf16[56,512]{1,0:T(8,128)(2,1)S(1)} %collective-permute-done.27.refs_3_) | copy-start | bytes 172036
  219.2 9.6 %collective-permute-start.23 = (bf16[56,512]{1,0:T(8,128)(2,1)S(1)}, bf16[56,512]{1,0:T(8,128)(2,1)S(1)}, u32[]{:S(2)}, u32[]{:S(2)}) collective-permute-start(bf16[56,512]{1,0:T(8,128)(2,1)S(1)} %get-tuple-element.122), channel_id=1, source_target_pairs={{0,8},{8,16},{16,24},{24,0},{1,9},{9,17},{17,25},{25,1},{2,10},{10... | collective-permute-start | bytes 172040 | tf_op jit(solution)/shard_map/ppermute | solution.py:805
  220.7 11.5 %copy-start.9 = (bf16[56,512]{1,0:T(8,128)(2,1)}, bf16[56,512]{1,0:T(8,128)(2,1)S(1)}, u32[]{:S(2)}) copy-start(bf16[56,512]{1,0:T(8,128)(2,1)S(1)} %collective-permute-done.26.refs_2_) | copy-start | bytes 172036
  228.9 3.3 %copy-start.10 = (bf16[56,512]{1,0:T(8,128)(2,1)}, bf16[56,512]{1,0:T(8,128)(2,1)S(1)}, u32[]{:S(2)}) copy-start(bf16[56,512]{1,0:T(8,128)(2,1)S(1)} %collective-permute-done.23.refs_1_) | copy-start | bytes 172036
  228.9 3.3 %copy-start.5 = (bf16[152,512]{1,0:T(8,128)(2,1)}, bf16[152,512]{1,0:T(8,128)(2,1)S(1)}, u32[]{:S(2)}) copy-start(bf16[152,512]{1,0:T(8,128)(2,1)S(1)} %collective-permute-done.31.refs_7_) | copy-start | bytes 466948
  232.1 0.7 copy-start.6
  232.1 0.7 copy-start.7

commit v2 on v1

--- a/solution.py
+++ b/solution.py
@@ -876,7 +876,8 @@
     near, second_rows = lax.optimization_barrier((near, second_rows))
     first_blocks = (near, across(near, 1))
     first_blocks, second_rows = lax.optimization_barrier((first_blocks, second_rows))
-    others = [across(second_rows, bits) for bits in (2, 4, 6)] + [across(second_rows, 1)]
+    diagonal = across(second_rows, 6)
+    others = [across(second_rows, bits) for bits in (2, 4)] + [diagonal, across(second_rows, 1)]
     *kept, attn, total, weights, gains = attend(lengths, place, False, tokens, first_blocks)
     kept += [weights, gains]
     attn, total, others = lax.optimization_barrier((attn, total, others))
@@ -885,7 +886,7 @@
     output, middle_grad, numer_grad, total_grad, *parts = feed(
         place, False, tokens, attn, total, cotangent, second_blocks
     )
-    others = [across(parts[chip], bits) for chip, bits in ((1, 2), (2, 4), (3, 6))]
+    others = [across(parts[chip], bits) for chip, bits in ((3, 6), (2, 4), (1, 2))]
     grad_tokens, near, far = attend_back(
         lengths, place, False, tokens, middle_grad, numer_grad, total_grad, kept
     )

time: 235 us -> 236 us (level)
  transfers between devices with their start and end apart: 32 -> 32, of which waited for: 13 -> 14; matrix products, arithmetic and copies ran while one was open for 3% -> 3% of each run, Pallas kernels for 34% -> 34%
where the time goes in v2:
time: 236 us
  Pallas kernels  149 us (63%)
  starting transfers between devices  37.7 us (16%)
  waiting for transfers between devices  37.7 us (16%)
  other arithmetic  7.07 us (3%)
  local copies, waits for them, and re-layouts  3.06 us (1%)
    pallas_call x1, Pallas kernels, feed(): pl.pallas_call(functools.partial(feed_kernel, plain), grid=(rows // LEN,)...  65.3 us
    pallas_call x1, Pallas kernels, attend_back(): pl.pallas_call(functools.partial(attend_back_kernel, plain), grid=(count,...  47.9 us
    pallas_call x1, Pallas kernels, attend(): pl.pallas_call(functools.partial(attend_kernel, plain), grid=(count,), in...  32.1 us
    ppermute x12, starting transfers between devices, along(): return lax.ppermute(values, 'dp', [(i, (i + step) % 4) for i in range(4)])  21.8 us
    ppermute x12, waiting for transfers between devices, along(): return lax.ppermute(values, 'dp', [(i, (i + step) % 4) for i in range(4)])  20.5 us
    ppermute x20, waiting for transfers between devices, across(): return lax.ppermute(values, 'fsdp', [(i, i ^ bits) for i in range(8)])  17.2 us
    ppermute x20, starting transfers between devices, across(): return lax.ppermute(values, 'fsdp', [(i, i ^ bits) for i in range(8)])  15.9 us
  transfers between devices with their start and end apart: 32, of which 14 were waited for; matrix products, arithmetic and copies ran while one was open for 3% of the time, Pallas kernels for 34%

profile of v2, /device:TPU:0, one launch (start us, length us, event | category | flops | bytes accessed | tf_op | source)
XLA Modules:
  0.0 235.8 jit_solution(11741688392809853502)
XLA Ops:
  0.6 0.6 pad_add_fusion.place
  1.3 1.8 pack.1
  3.1 5.0 %collective-permute-start.2 = (bf16[56,512]{1,0:T(8,128)(2,1)}, bf16[56,512]{1,0:T(8,128)(2,1)S(1)}, u32[]{:S(2)}, u32[]{:S(2)}) collective-permute-start(bf16[56,512]{1,0:T(8,128)(2,1)} %get-tuple-element.63), channel_id=1, source_target_pairs={{0,24},{8,0},{16,8},{24,16},{1,25},{9,1},{17,9},{25,17},{2,26},{10... | collective-permute-start | bytes 172040 | tf_op jit(solution)/shard_map/ppermute | solution.py:805
  8.1 1.0 collective-permute-start
  9.1 2.8 %collective-permute-start.8 = (bf16[152,512]{1,0:T(8,128)(2,1)}, bf16[152,512]{1,0:T(8,128)(2,1)S(1)}, u32[]{:S(2)}, u32[]{:S(2)}) collective-permute-start(bf16[152,512]{1,0:T(8,128)(2,1)} %get-tuple-element.64), channel_id=1, source_target_pairs={{0,24},{8,0},{16,8},{24,16},{1,25},{9,1},{17,9},{25,17},{2,26},{10... | collective-permute-start | bytes 466952 | tf_op jit(solution)/shard_map/ppermute | solution.py:805
  12.0 1.1 collective-permute-start.7
  13.1 0.8 constant_dynamic-update-slice_fusion.6
  13.9 0.0 collective-permute-start.6
  13.9 0.6 collective-permute-done.1
  14.5 0.5 collective-permute-done
  15.0 0.8 pad_maximum_fusion.1
  15.8 2.5 %collective-permute-start.5 = (bf16[4,56,512]{2,1,0:T(8,128)(2,1)S(1)}, bf16[4,56,512]{2,1,0:T(8,128)(2,1)S(1)}, u32[]{:S(2)}, u32[]{:S(2)}) collective-permute-start(bf16[4,56,512]{2,1,0:T(8,128)(2,1)S(1)} %pad_maximum_fusion.1), channel_id=1, source_target_pairs={{0,6},{1,7},{2,4},{3,5},{4,2},{5,3},{6,0},{7,1},{8,14},{9,15},{10,... | collective-permute-start | bytes 688136 | tf_op jit(solution)/shard_map/ppermute | solution.py:801
  18.3 0.5 collective-permute-start.3
  18.9 0.6 collective-permute-start.4
  19.5 8.0 %collective-permute-done.7 = bf16[152,512]{1,0:T(8,128)(2,1)S(1)} collective-permute-done((bf16[152,512]{1,0:T(8,128)(2,1)}, bf16[152,512]{1,0:T(8,128)(2,1)S(1)}, u32[]{:S(2)}, u32[]{:S(2)}) %collective-permute-start.7) | collective-permute-done | bytes 155680 | tf_op jit(solution)/shard_map/ppermute | solution.py:805
  27.5 1.0 pad_maximum_fusion.refs_0_
  28.6 0.0 copy-start.2
  28.6 0.1 collective-permute-start.9
  28.7 2.5 %collective-permute-done.9.far_blocks = bf16[16,56,512]{2,1,0:T(8,128)(2,1)S(1)} collective-permute-done((bf16[16,56,512]{2,1,0:T(8,128)(2,1)S(1)}, bf16[16,56,512]{2,1,0:T(8,128)(2,1)S(1)}, u32[]{:S(2)}, u32[]{:S(2)}) %collective-permute-start.9) | collective-permute-done | bytes 917536 | tf_op jit(solution)/shard_map/ppermute | solution.py:801
  31.2 0.1 collective-permute-start.13
  31.3 2.5 %collective-permute-start.12 = (bf16[4,152,512]{2,1,0:T(8,128)(2,1)S(1)}, bf16[4,152,512]{2,1,0:T(8,128)(2,1)}, u32[]{:S(2)}, u32[]{:S(2)}) collective-permute-start(bf16[4,152,512]{2,1,0:T(8,128)(2,1)S(1)} %pad_maximum_fusion.refs_0_), channel_id=1, source_target_pairs={{0,6},{1,7},{2,4},{3,5},{4,2},{5,3},{6,0},{7,1},{8,14},{9,15},{10,... | collective-permute-start | bytes 1867784 | tf_op jit(solution)/shard_map/ppermute | solution.py:801
  33.8 0.5 collective-permute-start.11
  34.3 0.5 collective-permute-start.10
  34.8 32.1 %attend.1 = (bf16[3,2192,512]{2,1,0:T(8,128)(2,1)}, bf16[3,2192,512]{2,1,0:T(8,128)(2,1)}, bf16[3,2192,512]{2,1,0:T(8,128)(2,1)}, bf16[3,4096,512]{2,1,0:T(8,128...) custom-call(s32[3]{0:T(128)} %lengths.3, ...), custom_call_target="tpu_custom_call" | custom-call | flops 40000000000 | bytes 40000000 | tf_op jit(solution)/shard_map/attend/pallas_call | solution.py:626
  67.0 0.1 collective-permute-start.14
  67.1 0.5 collective-permute-start.15
  67.6 0.1 collective-permute-start.16
  67.7 1.8 collective-permute-done.14.refs_5_
  69.4 0.9 collective-permute-done.15.refs_6_
  70.3 0.9 collective-permute-done.16.refs_7_
  71.2 65.3 %feed.1 = (bf16[3072,512]{1,0:T(8,128)(2,1)}, bf16[3072,512]{1,0:T(8,128)(2,1)}, bf16[3072,512]{1,0:T(8,128)(2,1)}, bf16[3072,512]{1,0:T(8,128)(2,1)}, bf16[8,15...) custom-call(s32[2]{0:T(128)} %pad_add_fusion.place, ...), custom_call_target="tpu_custom_call" | custom-call | flops 74999996416 | bytes 75000000 | tf_op jit(solution)/shard_map/feed/pallas_call | solution.py:679
  136.5 2.5 %collective-permute-start.18 = (bf16[8,152,512]{2,1,0:T(8,128)(2,1)}, bf16[8,152,512]{2,1,0:T(8,128)(2,1)}, u32[]{:S(2)}, u32[]{:S(2)}) collective-permute-start(bf16[8,152,512]{2,1,0:T(8,128)(2,1)} %get-tuple-element.91), channel_id=1, source_target_pairs={{0,6},{1,7},{2,4},{3,5},{4,2},{5,3},{6,0},{7,1},{8,14},{9,15},{10,... | collective-permute-start | bytes 3735560 | tf_op jit(solution)/shard_map/ppermute | solution.py:801
  139.0 0.5 collective-permute-start.19
  139.5 0.5 collective-permute-start.20
  140.1 47.9 %attend_back.1 = (bf16[3072,512]{1,0:T(8,128)(2,1)}, bf16[16,56,512]{2,1,0:T(8,128)(2,1)}, bf16[16,56,512]{2,1,0:T(8,128)(2,1)}) custom-call(s32[3]{0:T(128)} %lengths.3, s32[2]{0:T(128)} %pad_add_fusion.place, bf16[3072,512]{1,0:T(8,128)(2,1)} %tokens.5, bf16[3072,512]{1,0:T(8,128)(2,1)} %get-tuple-element.79.middle_grad, ...), custom_call_target="tpu_custom_call" | custom-call | flops 60000002048 | bytes 60000000 | tf_op jit(solution)/shard_map/attend_back/pallas_call | solution.py:715
  188.0 0.1 collective-permute-start.17
  188.0 2.7 %collective-permute-done.17 = bf16[16,56,512]{2,1,0:T(8,128)(2,1)S(1)} collective-permute-done((bf16[16,56,512]{2,1,0:T(8,128)(2,1)}, bf16[16,56,512]{2,1,0:T(8,128)(2,1)S(1)}, u32[]{:S(2)}, u32[]{:S(2)}) %collective-permute-start.17) | collective-permute-done | bytes 917536 | tf_op jit(solution)/shard_map/ppermute | solution.py:801
  190.7 3.2 %collective-permute-done.19 = bf16[8,152,512]{2,1,0:T(8,128)(2,1)} collective-permute-done((bf16[8,152,512]{2,1,0:T(8,128)(2,1)}, bf16[8,152,512]{2,1,0:T(8,128)(2,1)}, u32[]{:S(2)}, u32[]{:S(2)}) %collective-permute-start.19) | collective-permute-done | bytes 1245216 | tf_op jit(solution)/shard_map/ppermute | solution.py:801
  193.9 0.1 collective-permute-done.20
  194.0 1.5 add_convert_fusion.1
  195.6 1.5 collective-permute-start.24
  197.1 0.8 collective-permute-start.21
  198.0 2.7 %add_convert_fusion = bf16[8,152,512]{2,1,0:T(8,128)(2,1)S(1)} fusion(bf16[8,152,512]{2,1,0:T(8,128)(2,1)} %collective-permute-done.20, bf16[8,152,512]{2,1,0:T(8,128)(2,1)} %collective-permute-done.19, bf16[8,152,512]{2,1,0:T(8,128)(2,1)} %collective-permute-done.18, bf16[8,152,512]{2,1,0:T(8,128)(2,1)S(1)} %copy-done), kind=kLoop, calls=%fused_computation | loop fusion | flops 4980736 | bytes 6225920 | tf_op jit(solution)/shard_map/convert_element_type | solution.py:895
  200.7 0.1 collective-permute-start.28
  200.8 2.3 collective-permute-done.24
  203.1 0.1 add_convert_fusion.3
  203.2 1.6 collective-permute-start.25
  204.7 0.1 add_convert_fusion.4
  204.8 0.4 collective-permute-start.22
  205.2 2.9 %collective-permute-done.25 = bf16[2,56,512]{2,1,0:T(8,128)(2,1)S(1)} collective-permute-done((bf16[2,56,512]{2,1,0:T(8,128)(2,1)S(1)}, bf16[2,56,512]{2,1,0:T(8,128)(2,1)S(1)}, u32[]{:S(2)}, u32[]{:S(2)}) %collective-permute-start.25) | collective-permute-done | bytes 114720 | tf_op jit(solution)/shard_map/ppermute | solution.py:801
  208.1 1.8 collective-permute-start.27
  209.9 5.1 %collective-permute-start.26 = (bf16[56,512]{1,0:T(8,128)(2,1)S(1)}, bf16[56,512]{1,0:T(8,128)(2,1)S(1)}, u32[]{:S(2)}, u32[]{:S(2)}) collective-permute-start(bf16[56,512]{1,0:T(8,128)(2,1)S(1)} %get-tuple-element.121), channel_id=1, source_target_pairs={{0,16},{8,24},{16,0},{24,8},{1,17},{9,25},{17,1},{25,9},{2,18},{10... | collective-permute-start | bytes 172040 | tf_op jit(solution)/shard_map/ppermute | solution.py:805
  215.0 0.2 add_convert_fusion.2
  215.2 0.7 slice_bitcast_fusion
  215.9 1.4 collective-permute-start.31
  217.3 2.0 collective-permute-start.30
  219.3 0.1 collective-permute-start.29
  219.4 0.6 slice_bitcast_fusion.10
  220.0 1.4 collective-permute-start.23
  221.4 8.5 %collective-permute-done.23.refs_1_ = bf16[56,512]{1,0:T(8,128)(2,1)S(1)} collective-permute-done((bf16[56,512]{1,0:T(8,128)(2,1)S(1)}, bf16[56,512]{1,0:T(8,128)(2,1)S(1)}, u32[]{:S(2)}, u32[]{:S(2)}) %collective-permute-start.23) | collective-permute-done | bytes 57376 | tf_op jit(solution)/shard_map/ppermute | solution.py:805
  229.9 3.0 %collective-permute-done.30.refs_6_ = bf16[152,512]{1,0:T(8,128)(2,1)S(1)} collective-permute-done((bf16[152,512]{1,0:T(8,128)(2,1)S(1)}, bf16[152,512]{1,0:T(8,128)(2,1)S(1)}, u32[]{:S(2)}, u32[]{:S(2)}) %collective-permute-start.30) | collective-permute-done | bytes 155680 | tf_op jit(solution)/shard_map/ppermute | solution.py:805
  232.9 0.6 copy-done.6
  233.5 0.1 copy-done.7
  233.6 2.0 finish.1
  (53 shorter events, 0.4 us)
Async XLA Ops:
  3.1 10.8 %collective-permute-start.2 = (bf16[56,512]{1,0:T(8,128)(2,1)}, bf16[56,512]{1,0:T(8,128)(2,1)S(1)}, u32[]{:S(2)}, u32[]{:S(2)}) collective-permute-start(bf16[56,512]{1,0:T(8,128)(2,1)} %get-tuple-element.63), channel_id=1, source_target_pairs={{0,24},{8,0},{16,8},{24,16},{1,25},{9,1},{17,9},{25,17},{2,26},{10... | collective-permute-start | bytes 172040 | tf_op jit(solution)/shard_map/ppermute | solution.py:805
  8.1 6.4 %collective-permute-start.1 = (bf16[56,512]{1,0:T(8,128)(2,1)}, bf16[56,512]{1,0:T(8,128)(2,1)S(1)}, u32[]{:S(2)}, u32[]{:S(2)}) collective-permute-start(bf16[56,512]{1,0:T(8,128)(2,1)} %get-tuple-element.63), channel_id=1, source_target_pairs={{0,16},{8,24},{16,0},{24,8},{1,17},{9,25},{17,1},{25,9},{2,18},{10... | collective-permute-start | bytes 172040 | tf_op jit(solution)/shard_map/ppermute | solution.py:805
  8.1 6.9 %collective-permute-start = (bf16[56,512]{1,0:T(8,128)(2,1)}, bf16[56,512]{1,0:T(8,128)(2,1)S(1)}, u32[]{:S(2)}, u32[]{:S(2)}) collective-permute-start(bf16[56,512]{1,0:T(8,128)(2,1)} %get-tuple-element.63), channel_id=1, source_target_pairs={{0,8},{8,16},{16,24},{24,0},{1,9},{9,17},{17,25},{25,1},{2,10},{10... | collective-permute-start | bytes 172040 | tf_op jit(solution)/shard_map/ppermute | solution.py:805
  9.1 9.8 %collective-permute-start.8 = (bf16[152,512]{1,0:T(8,128)(2,1)}, bf16[152,512]{1,0:T(8,128)(2,1)S(1)}, u32[]{:S(2)}, u32[]{:S(2)}) collective-permute-start(bf16[152,512]{1,0:T(8,128)(2,1)} %get-tuple-element.64), channel_id=1, source_target_pairs={{0,24},{8,0},{16,8},{24,16},{1,25},{9,1},{17,9},{25,17},{2,26},{10... | collective-permute-start | bytes 466952 | tf_op jit(solution)/shard_map/ppermute | solution.py:805
  12.0 15.5 %collective-permute-start.7 = (bf16[152,512]{1,0:T(8,128)(2,1)}, bf16[152,512]{1,0:T(8,128)(2,1)S(1)}, u32[]{:S(2)}, u32[]{:S(2)}) collective-permute-start(bf16[152,512]{1,0:T(8,128)(2,1)} %get-tuple-element.64), channel_id=1, source_target_pairs={{0,16},{8,24},{16,0},{24,8},{1,17},{9,25},{17,1},{25,9},{2,18},{10... | collective-permute-start | bytes 466952 | tf_op jit(solution)/shard_map/ppermute | solution.py:805
  13.9 13.6 %collective-permute-start.6 = (bf16[152,512]{1,0:T(8,128)(2,1)}, bf16[152,512]{1,0:T(8,128)(2,1)S(1)}, u32[]{:S(2)}, u32[]{:S(2)}) collective-permute-start(bf16[152,512]{1,0:T(8,128)(2,1)} %get-tuple-element.64), channel_id=1, source_target_pairs={{0,8},{8,16},{16,24},{24,0},{1,9},{9,17},{17,25},{25,1},{2,10},{10... | collective-permute-start | bytes 466952 | tf_op jit(solution)/shard_map/ppermute | solution.py:805
  15.8 12.7 %collective-permute-start.5 = (bf16[4,56,512]{2,1,0:T(8,128)(2,1)S(1)}, bf16[4,56,512]{2,1,0:T(8,128)(2,1)S(1)}, u32[]{:S(2)}, u32[]{:S(2)}) collective-permute-start(bf16[4,56,512]{2,1,0:T(8,128)(2,1)S(1)} %pad_maximum_fusion.1), channel_id=1, source_target_pairs={{0,6},{1,7},{2,4},{3,5},{4,2},{5,3},{6,0},{7,1},{8,14},{9,15},{10,... | collective-permute-start | bytes 688136 | tf_op jit(solution)/shard_map/ppermute | solution.py:801
  18.3 10.2 %collective-permute-start.3 = (bf16[4,56,512]{2,1,0:T(8,128)(2,1)S(1)}, bf16[4,56,512]{2,1,0:T(8,128)(2,1)S(1)}, u32[]{:S(2)}, u32[]{:S(2)}) collective-permute-start(bf16[4,56,512]{2,1,0:T(8,128)(2,1)S(1)} %pad_maximum_fusion.1), channel_id=1, source_target_pairs={{0,2},{1,3},{2,0},{3,1},{4,6},{5,7},{6,4},{7,5},{8,10},{9,11},{10,... | collective-permute-start | bytes 688136 | tf_op jit(solution)/shard_map/ppermute | solution.py:801
  18.9 9.6 %collective-permute-start.4 = (bf16[4,56,512]{2,1,0:T(8,128)(2,1)S(1)}, bf16[4,56,512]{2,1,0:T(8,128)(2,1)S(1)}, u32[]{:S(2)}, u32[]{:S(2)}) collective-permute-start(bf16[4,56,512]{2,1,0:T(8,128)(2,1)S(1)} %pad_maximum_fusion.1), channel_id=1, source_target_pairs={{0,4},{1,5},{2,6},{3,7},{4,0},{5,1},{6,2},{7,3},{8,12},{9,13},{10,... | collective-permute-start | bytes 688136 | tf_op jit(solution)/shard_map/ppermute | solution.py:801
  28.5 38.5 %copy-start.1 = (bf16[4,152,512]{2,1,0:T(8,128)(2,1)}, bf16[4,152,512]{2,1,0:T(8,128)(2,1)S(1)}, u32[]{:S(2)}) copy-start(bf16[4,152,512]{2,1,0:T(8,128)(2,1)S(1)} %pad_maximum_fusion.refs_0_) | copy-start | bytes 1867780
  28.6 5.2 %copy-start.2 = (bf16[16,56,512]{2,1,0:T(8,128)(2,1)}, bf16[16,56,512]{2,1,0:T(8,128)(2,1)S(1)}, u32[]{:S(2)}) copy-start(bf16[16,56,512]{2,1,0:T(8,128)(2,1)S(1)} %constant_dynamic-update-slice_fusion.near_blocks) | copy-start | bytes 2752516
  28.6 2.5 %collective-permute-start.9 = (bf16[16,56,512]{2,1,0:T(8,128)(2,1)S(1)}, bf16[16,56,512]{2,1,0:T(8,128)(2,1)S(1)}, u32[]{:S(2)}, u32[]{:S(2)}) collective-permute-start(bf16[16,56,512]{2,1,0:T(8,128)(2,1)S(1)} %constant_dynamic-update-slice_fusion.near_blocks), channel_id=1, source_target_pairs={{0,1},{1,0},{2,3},{3,2},{4,5},{5,4},{6,7},{7,6},{8,9},{9,8},{10,11... | collective-permute-start | bytes 2752520 | tf_op jit(solution)/shard_map/ppermute | solution.py:801
  31.2 3.1 %copy-start.3 = (bf16[16,56,512]{2,1,0:T(8,128)(2,1)}, bf16[16,56,512]{2,1,0:T(8,128)(2,1)S(1)}, u32[]{:S(2)}) copy-start(bf16[16,56,512]{2,1,0:T(8,128)(2,1)S(1)} %collective-permute-done.9.far_blocks) | copy-start | bytes 2752516
  31.2 35.8 %collective-permute-start.13 = (bf16[4,152,512]{2,1,0:T(8,128)(2,1)S(1)}, bf16[4,152,512]{2,1,0:T(8,128)(2,1)}, u32[]{:S(2)}, u32[]{:S(2)}) collective-permute-start(bf16[4,152,512]{2,1,0:T(8,128)(2,1)S(1)} %pad_maximum_fusion.refs_0_), channel_id=1, source_target_pairs={{0,1},{1,0},{2,3},{3,2},{4,5},{5,4},{6,7},{7,6},{8,9},{9,8},{10,11... | collective-permute-start | bytes 1867784 | tf_op jit(solution)/shard_map/ppermute | solution.py:801
  31.3 35.7 %collective-permute-start.12 = (bf16[4,152,512]{2,1,0:T(8,128)(2,1)S(1)}, bf16[4,152,512]{2,1,0:T(8,128)(2,1)}, u32[]{:S(2)}, u32[]{:S(2)}) collective-permute-start(bf16[4,152,512]{2,1,0:T(8,128)(2,1)S(1)} %pad_maximum_fusion.refs_0_), channel_id=1, source_target_pairs={{0,6},{1,7},{2,4},{3,5},{4,2},{5,3},{6,0},{7,1},{8,14},{9,15},{10,... | collective-permute-start | bytes 1867784 | tf_op jit(solution)/shard_map/ppermute | solution.py:801
  33.8 33.2 %collective-permute-start.11 = (bf16[4,152,512]{2,1,0:T(8,128)(2,1)S(1)}, bf16[4,152,512]{2,1,0:T(8,128)(2,1)}, u32[]{:S(2)}, u32[]{:S(2)}) collective-permute-start(bf16[4,152,512]{2,1,0:T(8,128)(2,1)S(1)} %pad_maximum_fusion.refs_0_), channel_id=1, source_target_pairs={{0,4},{1,5},{2,6},{3,7},{4,0},{5,1},{6,2},{7,3},{8,12},{9,13},{10,... | collective-permute-start | bytes 1867784 | tf_op jit(solution)/shard_map/ppermute | solution.py:801
  34.3 32.7 %collective-permute-start.10 = (bf16[4,152,512]{2,1,0:T(8,128)(2,1)S(1)}, bf16[4,152,512]{2,1,0:T(8,128)(2,1)}, u32[]{:S(2)}, u32[]{:S(2)}) collective-permute-start(bf16[4,152,512]{2,1,0:T(8,128)(2,1)S(1)} %pad_maximum_fusion.refs_0_), channel_id=1, source_target_pairs={{0,2},{1,3},{2,0},{3,1},{4,6},{5,7},{6,4},{7,5},{8,10},{9,11},{10,... | collective-permute-start | bytes 1867784 | tf_op jit(solution)/shard_map/ppermute | solution.py:801
  67.0 2.4 %collective-permute-start.14 = (bf16[4,152,512]{2,1,0:T(8,128)(2,1)}, bf16[4,152,512]{2,1,0:T(8,128)(2,1)S(1)}, u32[]{:S(2)}, u32[]{:S(2)}) collective-permute-start(bf16[4,152,512]{2,1,0:T(8,128)(2,1)} %collective-permute-done.10.refs_1_), channel_id=1, source_target_pairs={{0,1},{1,0},{2,3},{3,2},{4,5},{5,4},{6,7},{7,6},{8,9},{9,8},{10,11... | collective-permute-start | bytes 1867784 | tf_op jit(solution)/shard_map/ppermute | solution.py:801
  67.1 3.3 %collective-permute-start.15 = (bf16[4,152,512]{2,1,0:T(8,128)(2,1)}, bf16[4,152,512]{2,1,0:T(8,128)(2,1)}, u32[]{:S(2)}, u32[]{:S(2)}) collective-permute-start(bf16[4,152,512]{2,1,0:T(8,128)(2,1)} %collective-permute-done.11.refs_2_), channel_id=1, source_target_pairs={{0,1},{1,0},{2,3},{3,2},{4,5},{5,4},{6,7},{7,6},{8,9},{9,8},{10,11... | collective-permute-start | bytes 1867784 | tf_op jit(solution)/shard_map/ppermute | solution.py:801
  67.6 3.7 %collective-permute-start.16 = (bf16[4,152,512]{2,1,0:T(8,128)(2,1)}, bf16[4,152,512]{2,1,0:T(8,128)(2,1)}, u32[]{:S(2)}, u32[]{:S(2)}) collective-permute-start(bf16[4,152,512]{2,1,0:T(8,128)(2,1)} %collective-permute-done.12.refs_3_), channel_id=1, source_target_pairs={{0,1},{1,0},{2,3},{3,2},{4,5},{5,4},{6,7},{7,6},{8,9},{9,8},{10,11... | collective-permute-start | bytes 1867784 | tf_op jit(solution)/shard_map/ppermute | solution.py:801
  69.4 1.8 copy-start.4
  136.5 54.2 %collective-permute-start.18 = (bf16[8,152,512]{2,1,0:T(8,128)(2,1)}, bf16[8,152,512]{2,1,0:T(8,128)(2,1)}, u32[]{:S(2)}, u32[]{:S(2)}) collective-permute-start(bf16[8,152,512]{2,1,0:T(8,128)(2,1)} %get-tuple-element.91), channel_id=1, source_target_pairs={{0,6},{1,7},{2,4},{3,5},{4,2},{5,3},{6,0},{7,1},{8,14},{9,15},{10,... | collective-permute-start | bytes 3735560 | tf_op jit(solution)/shard_map/ppermute | solution.py:801
  139.0 54.8 %collective-permute-start.19 = (bf16[8,152,512]{2,1,0:T(8,128)(2,1)}, bf16[8,152,512]{2,1,0:T(8,128)(2,1)}, u32[]{:S(2)}, u32[]{:S(2)}) collective-permute-start(bf16[8,152,512]{2,1,0:T(8,128)(2,1)} %get-tuple-element.92), channel_id=1, source_target_pairs={{0,4},{1,5},{2,6},{3,7},{4,0},{5,1},{6,2},{7,3},{8,12},{9,13},{10,... | collective-permute-start | bytes 3735560 | tf_op jit(solution)/shard_map/ppermute | solution.py:801
  139.5 54.5 %collective-permute-start.20 = (bf16[8,152,512]{2,1,0:T(8,128)(2,1)}, bf16[8,152,512]{2,1,0:T(8,128)(2,1)}, u32[]{:S(2)}, u32[]{:S(2)}) collective-permute-start(bf16[8,152,512]{2,1,0:T(8,128)(2,1)} %get-tuple-element.93), channel_id=1, source_target_pairs={{0,2},{1,3},{2,0},{3,1},{4,6},{5,7},{6,4},{7,5},{8,10},{9,11},{10,... | collective-permute-start | bytes 3735560 | tf_op jit(solution)/shard_map/ppermute | solution.py:801
  188.0 2.7 %collective-permute-start.17 = (bf16[16,56,512]{2,1,0:T(8,128)(2,1)}, bf16[16,56,512]{2,1,0:T(8,128)(2,1)S(1)}, u32[]{:S(2)}, u32[]{:S(2)}) collective-permute-start(bf16[16,56,512]{2,1,0:T(8,128)(2,1)} %get-tuple-element.90), channel_id=1, source_target_pairs={{0,1},{1,0},{2,3},{3,2},{4,5},{5,4},{6,7},{7,6},{8,9},{9,8},{10,11... | collective-permute-start | bytes 2752520 | tf_op jit(solution)/shard_map/ppermute | solution.py:801
  194.0 4.0 %copy-start = (bf16[8,152,512]{2,1,0:T(8,128)(2,1)S(1)}, bf16[8,152,512]{2,1,0:T(8,128)(2,1)}, u32[]{:S(2)}) copy-start(bf16[8,152,512]{2,1,0:T(8,128)(2,1)} %get-tuple-element.96) | copy-start | bytes 3735556
  195.6 7.5 %collective-permute-start.24 = (bf16[2,2,56,512]{3,2,1,0:T(8,128)(2,1)S(1)}, bf16[2,2,56,512]{3,2,1,0:T(8,128)(2,1)S(1)}, u32[]{:S(2)}, u32[]{:S(2)}) collective-permute-start(bf16[2,2,56,512]{3,2,1,0:T(8,128)(2,1)S(1)} %stack.69), channel_id=1, source_target_pairs={{0,4},{1,5},{2,6},{3,7},{4,0},{5,1},{6,2},{7,3},{8,12},{9,13},{10,... | collective-permute-start | bytes 688136 | tf_op jit(solution)/shard_map/ppermute | solution.py:801
  197.1 7.6 %collective-permute-start.21 = (bf16[2,2,56,512]{3,2,1,0:T(8,128)(2,1)S(1)}, bf16[2,2,56,512]{3,2,1,0:T(8,128)(2,1)S(1)}, u32[]{:S(2)}, u32[]{:S(2)}) collective-permute-start(bf16[2,2,56,512]{3,2,1,0:T(8,128)(2,1)S(1)} %pad_maximum_fusion.2), channel_id=1, source_target_pairs={{0,2},{1,3},{2,0},{3,1},{4,6},{5,7},{6,4},{7,5},{8,10},{9,11},{10,... | collective-permute-start | bytes 688136 | tf_op jit(solution)/shard_map/ppermute | solution.py:801
  200.7 14.3 %collective-permute-start.28 = (bf16[4,152,512]{2,1,0:T(8,128)(2,1)S(1)}, bf16[4,152,512]{2,1,0:T(8,128)(2,1)S(1)}, u32[]{:S(2)}, u32[]{:S(2)}) collective-permute-start(bf16[4,152,512]{2,1,0:T(8,128)(2,1)S(1)} %slice.101), channel_id=1, source_target_pairs={{0,1},{1,0},{2,3},{3,2},{4,5},{5,4},{6,7},{7,6},{8,9},{9,8},{10,11... | collective-permute-start | bytes 1867784 | tf_op jit(solution)/shard_map/ppermute | solution.py:801
  203.2 4.9 %collective-permute-start.25 = (bf16[2,56,512]{2,1,0:T(8,128)(2,1)S(1)}, bf16[2,56,512]{2,1,0:T(8,128)(2,1)S(1)}, u32[]{:S(2)}, u32[]{:S(2)}) collective-permute-start(bf16[2,56,512]{2,1,0:T(8,128)(2,1)S(1)} %slice_bitcast_fusion.4), channel_id=1, source_target_pairs={{0,2},{1,3},{2,0},{3,1},{4,6},{5,7},{6,4},{7,5},{8,10},{9,11},{10,... | collective-permute-start | bytes 344072 | tf_op jit(solution)/shard_map/ppermute | solution.py:801
  204.8 10.2 %collective-permute-start.22 = (bf16[2,56,512]{2,1,0:T(8,128)(2,1)S(1)}, bf16[2,56,512]{2,1,0:T(8,128)(2,1)S(1)}, u32[]{:S(2)}, u32[]{:S(2)}) collective-permute-start(bf16[2,56,512]{2,1,0:T(8,128)(2,1)S(1)} %slice_bitcast_fusion.6), channel_id=1, source_target_pairs={{0,4},{1,5},{2,6},{3,7},{4,0},{5,1},{6,2},{7,3},{8,12},{9,13},{10,... | collective-permute-start | bytes 344072 | tf_op jit(solution)/shard_map/ppermute | solution.py:801
  208.1 11.9 %collective-permute-start.27 = (bf16[56,512]{1,0:T(8,128)(2,1)S(1)}, bf16[56,512]{1,0:T(8,128)(2,1)S(1)}, u32[]{:S(2)}, u32[]{:S(2)}) collective-permute-start(bf16[56,512]{1,0:T(8,128)(2,1)S(1)} %get-tuple-element.120), channel_id=1, source_target_pairs={{0,24},{8,0},{16,8},{24,16},{1,25},{9,1},{17,9},{25,17},{2,26},{10... | collective-permute-start | bytes 172040 | tf_op jit(solution)/shard_map/ppermute | solution.py:805
  209.9 11.6 %collective-permute-start.26 = (bf16[56,512]{1,0:T(8,128)(2,1)S(1)}, bf16[56,512]{1,0:T(8,128)(2,1)S(1)}, u32[]{:S(2)}, u32[]{:S(2)}) collective-permute-start(bf16[56,512]{1,0:T(8,128)(2,1)S(1)} %get-tuple-element.121), channel_id=1, source_target_pairs={{0,16},{8,24},{16,0},{24,8},{1,17},{9,25},{17,1},{25,9},{2,18},{10... | collective-permute-start | bytes 172040 | tf_op jit(solution)/shard_map/ppermute | solution.py:805
  215.9 14.0 %collective-permute-start.31 = (bf16[152,512]{1,0:T(8,128)(2,1)S(1)}, bf16[152,512]{1,0:T(8,128)(2,1)S(1)}, u32[]{:S(2)}, u32[]{:S(2)}) collective-permute-start(bf16[152,512]{1,0:T(8,128)(2,1)S(1)} %get-tuple-element.116), channel_id=1, source_target_pairs={{0,24},{8,0},{16,8},{24,16},{1,25},{9,1},{17,9},{25,17},{2,26},{10... | collective-permute-start | bytes 466952 | tf_op jit(solution)/shard_map/ppermute | solution.py:805
  217.3 15.6 %collective-permute-start.30 = (bf16[152,512]{1,0:T(8,128)(2,1)S(1)}, bf16[152,512]{1,0:T(8,128)(2,1)S(1)}, u32[]{:S(2)}, u32[]{:S(2)}) collective-permute-start(bf16[152,512]{1,0:T(8,128)(2,1)S(1)} %get-tuple-element.117), channel_id=1, source_target_pairs={{0,16},{8,24},{16,0},{24,8},{1,17},{9,25},{17,1},{25,9},{2,18},{10... | collective-permute-start | bytes 466952 | tf_op jit(solution)/shard_map/ppermute | solution.py:805
  219.3 13.6 %collective-permute-start.29 = (bf16[152,512]{1,0:T(8,128)(2,1)S(1)}, bf16[152,512]{1,0:T(8,128)(2,1)S(1)}, u32[]{:S(2)}, u32[]{:S(2)}) collective-permute-start(bf16[152,512]{1,0:T(8,128)(2,1)S(1)} %get-tuple-element.118), channel_id=1, source_target_pairs={{0,8},{8,16},{16,24},{24,0},{1,9},{9,17},{17,25},{25,1},{2,10},{10... | collective-permute-start | bytes 466952 | tf_op jit(solution)/shard_map/ppermute | solution.py:805
  220.0 12.9 %copy-start.8 = (bf16[56,512]{1,0:T(8,128)(2,1)}, bf16[56,512]{1,0:T(8,128)(2,1)S(1)}, u32[]{:S(2)}) copy-start(bf16[56,512]{1,0:T(8,128)(2,1)S(1)} %collective-permute-done.27.refs_3_) | copy-start | bytes 172036
  220.0 9.9 %collective-permute-start.23 = (bf16[56,512]{1,0:T(8,128)(2,1)S(1)}, bf16[56,512]{1,0:T(8,128)(2,1)S(1)}, u32[]{:S(2)}, u32[]{:S(2)}) collective-permute-start(bf16[56,512]{1,0:T(8,128)(2,1)S(1)} %get-tuple-element.122), channel_id=1, source_target_pairs={{0,8},{8,16},{16,24},{24,0},{1,9},{9,17},{17,25},{25,1},{2,10},{10... | collective-permute-start | bytes 172040 | tf_op jit(solution)/shard_map/ppermute | solution.py:805
  221.4 11.5 %copy-start.9 = (bf16[56,512]{1,0:T(8,128)(2,1)}, bf16[56,512]{1,0:T(8,128)(2,1)S(1)}, u32[]{:S(2)}) copy-start(bf16[56,512]{1,0:T(8,128)(2,1)S(1)} %collective-permute-done.26.refs_2_) | copy-start | bytes 172036
  229.9 3.0 %copy-start.10 = (bf16[56,512]{1,0:T(8,128)(2,1)}, bf16[56,512]{1,0:T(8,128)(2,1)S(1)}, u32[]{:S(2)}) copy-start(bf16[56,512]{1,0:T(8,128)(2,1)S(1)} %collective-permute-done.23.refs_1_) | copy-start | bytes 172036
  229.9 3.0 %copy-start.5 = (bf16[152,512]{1,0:T(8,128)(2,1)}, bf16[152,512]{1,0:T(8,128)(2,1)S(1)}, u32[]{:S(2)}) copy-start(bf16[152,512]{1,0:T(8,128)(2,1)S(1)} %collective-permute-done.31.refs_7_) | copy-start | bytes 466948
  232.9 0.7 copy-start.6
  232.9 0.7 copy-start.7
